TPU v7x, 32 devices: a whole 2x2x4 slice. The times are simulated.
32 devices in a mesh: gx: 8 (over z, y), gy: 4 (over x, core).
Axes of the slice: x: 2, y: 2, z: 4, core: 2. Of those that a mesh axis runs over, the one named last changes fastest.
Arguments:
- rhs_field: float32 [3, 32, 32, 2048], P(None, None, 'gy', 'gx'), may hold values from -6 to 6
- couplings: float32 [6, 3, 3, 32, 32, 2048], P(None, None, None, None, 'gy', 'gx'), may hold values from -0.6 to 0.6
- pivot_inverses: float32 [3, 3, 32, 32, 2048], P(None, None, None, 'gy', 'gx'), may hold values from -3.5 to 3.5
- colours: int32 [32, 32, 2048], P(None, 'gy', 'gx'), may hold values from 0 to 3
- perf_cells: int32 [32768], P(('gx', 'gy')), may hold values from 0 to 65535
- perf_wells: int32 [32768], P(('gx', 'gy')), may hold values from 0 to 2047, as said below
- perf_segments: int32 [32768], P(('gx', 'gy')), may hold values from 0 to 15
- perf_gather: float32 [3, 32768], P(None, ('gx', 'gy')), may hold values from -3 to 3
- perf_return: float32 [3, 32768], P(None, ('gx', 'gy')), may hold values from -3 to 3
- well_slot: int32 [2048], replicated, may hold values from 0 to 2047, as said below
- seg_count: int32 [2048], replicated, may hold values from 1 to 16
- well_inverses: float32 [2048, 16, 16], P(('gx', 'gy')), may hold values from -1.5 to 1.5
Outputs:
- precond_field: float32 [3, 32, 32, 2048], P(None, None, 'gy', 'gx')
Inputs may be any that keep to these rules, and one draw needn't show every extreme that they name: `well_slot`: wells are numbered by owner: well w's slot lies in w // 64 * 64 to that plus 64 - 1, each slot taken once, so slot s belongs to tile s // 64 (tiles ordered with x slowest). `perf_wells`: A perforation listed with a tile may name a well of any owner.
All inputs are finite; a program needn't handle non-finite values.
Results may differ from a plain program's by a relative error of at most 0.0001.
Values sent between devices are 32-bit elements; how exact they have to be, the bound alone decides.
A program may use at most 384 MiB of HBM per device.

v0:
```python
import jax
import jax.numpy as jnp
from jax import lax
from jax.sharding import PartitionSpec as P


def padded_2(cells, sides, width):
    for axis, dim in sides:
        count = lax.axis_size(axis)
        ends = count - 1
        head = lax.slice_in_dim(cells, 0, width, axis=dim)
        tail = lax.slice_in_dim(cells, cells.shape[dim] - width, cells.shape[dim], axis=dim)
        cells = jnp.concatenate(
            [
                lax.ppermute(tail, axis, [(i, (i + 1) % count) for i in range(ends)]),
                cells,
                lax.ppermute(head, axis, [((i + 1) % count, i) for i in range(ends)]),
            ],
            axis=dim,
        )
    return cells


def gather_beside(couplings, padded_xy):
    padded = jnp.pad(padded_xy, ((0, 0), (1, 1), (0, 0), (0, 0)))
    beside = jnp.stack(
        [
            padded[:, 1:-1, 1:-1, :-2],
            padded[:, 1:-1, 1:-1, 2:],
            padded[:, 1:-1, :-2, 1:-1],
            padded[:, 1:-1, 2:, 1:-1],
            padded[:, :-2, 1:-1, 1:-1],
            padded[:, 2:, 1:-1, 1:-1],
        ]
    )
    return jnp.sum(couplings * beside[:, None], axis=(0, 2))


def couple_lower(couplings, field):
    padded_xy = padded_2(field, (("gx", 3), ("gy", 2)), 1)
    return gather_beside(couplings, padded_xy)


def couple_upper(couplings, field):
    padded_xy = padded_2(field, (("gx", 3), ("gy", 2)), 1)
    return gather_beside(couplings, padded_xy)


def pivot(pivot_inverses, field):
    return jnp.sum(pivot_inverses * field[None], axis=1)


def well_solve(inverses, totals, seg_counts):
    seg_index = jnp.arange(totals.shape[1], dtype=jnp.int32)
    alive_mask = (seg_index[None, :] < seg_counts[:, None]).astype(jnp.float32)
    return alive_mask * jnp.einsum(
        "wst,wt->ws", inverses, alive_mask * totals, precision=lax.Precision.HIGHEST
    )


def shards(
    rhs_field,
    couplings,
    pivot_inverses,
    colours,
    perf_cells,
    perf_wells,
    perf_segments,
    perf_gather,
    perf_return,
    well_slot,
    seg_count,
    well_inverses,
):
    segments = well_inverses.shape[1]
    wells_all = well_slot.shape[0]
    owned = well_inverses.shape[0]
    lower = jnp.zeros_like(rhs_field)
    upper_in = jnp.zeros_like(rhs_field)
    for colour in range(4):
        chosen = (colours == colour)[None]
        if colour == 0:
            current = rhs_field
        else:
            current = rhs_field - couple_lower(couplings, lower)
        upper_in = jnp.where(chosen, current, upper_in)
        lower = jnp.where(chosen, pivot(pivot_inverses, current), lower)
    sweep_field = jnp.zeros_like(rhs_field)
    for colour in (3, 2, 1, 0):
        chosen = (colours == colour)[None]
        if colour == 3:
            current = pivot(pivot_inverses, upper_in)
        else:
            current = pivot(pivot_inverses, upper_in - couple_upper(couplings, sweep_field))
        sweep_field = jnp.where(chosen, current, sweep_field)
    flat_field = sweep_field.reshape(3, -1)
    terms = jnp.sum(perf_gather * flat_field[:, perf_cells], axis=0)
    slots = well_slot[perf_wells]
    slot_counts = jnp.zeros((wells_all,), jnp.int32).at[well_slot].set(seg_count)
    well_key = slots * segments + perf_segments
    local_totals = (
        jnp.zeros((wells_all * segments,), jnp.float32)
        .at[well_key]
        .add(terms)
        .reshape(wells_all, segments)
    )
    own_totals = lax.psum_scatter(local_totals, ("gx", "gy"), scatter_dimension=0, tiled=True)
    own_counts = lax.dynamic_slice_in_dim(slot_counts, lax.axis_index(("gx", "gy")) * owned, owned)
    own_values = well_solve(well_inverses, own_totals, own_counts)
    values_all = lax.all_gather(own_values, ("gx", "gy"), axis=0, tiled=True)
    at_perfs = values_all.reshape(-1)[well_key]
    result = flat_field.at[:, perf_cells].add(-perf_return * at_perfs[None])
    return result.reshape(sweep_field.shape)


def solution(mesh):
    return jax.shard_map(
        shards,
        mesh=mesh,
        in_specs=(
            P(None, None, "gy", "gx"),
            P(None, None, None, None, "gy", "gx"),
            P(None, None, None, "gy", "gx"),
            P(None, "gy", "gx"),
            P(("gx", "gy")),
            P(("gx", "gy")),
            P(("gx", "gy")),
            P(None, ("gx", "gy")),
            P(None, ("gx", "gy")),
            P(),
            P(),
            P(("gx", "gy"), None, None),
        ),
        out_specs=P(None, None, "gy", "gx"),
        check_vma=False,
    )
```

profile of v0, /device:TPU:0, one launch (start us, length us, event | category | flops | bytes accessed | tf_op | source)
XLA Modules:
  0.0 678.2 jit_solution(963908049342525067)
XLA Ops:
  16.9 15.5 %collective-permute-done = f32[3,32,8,1]{3,2,1,0:T(8,128)S(1)} collective-permute-done((f32[3,32,8,1]{3,2,1,0:T(8,128)S(1)}, f32[3,32,8,1]{3,2,1,0:T(8,128)S(1)}, u32[]{:S(2)}, u32[]{:S(2)}) %collective-permute-start) | collective-permute-done | bytes 3104 | tf_op jit(solution)/shard_map/ppermute | solution.py:15
  44.3 9.3 %multiply_reduce_fusion.5 = f32[3,32,8,256]{3,2,1,0:T(8,128)} fusion(f32[6,3,3,32,8,256]{5,4,3,2,1,0:T(8,128)} %param.13, f32[6,3,32,8,256]{4,3,2,1,0:T(8,128)} %fusion.54), kind=kLoop, calls=%fused_computation.15 | loop fusion | flops 6881280 | bytes 19660800 | tf_op jit(solution)/shard_map/reduce_sum | solution.py:36
  61.6 5.4 collective-permute-done.4
  67.0 6.1 collective-permute-done.5
  73.9 7.2 %collective-permute-start.6 = (f32[3,32,1,258]{3,2,1,0:T(1,128)S(1)}, f32[3,32,1,258]{3,2,1,0:T(1,128)S(1)}, u32[]{:S(2)}, u32[]{:S(2)}) collective-permute-start(f32[3,32,1,258]{3,2,1,0:T(1,128)S(1)} %get-tuple-element.16), channel_id=1, source_target_pairs={{0,1},{1,2},{2,3},{4,5},{5,6},{6,7},{8,9},{9,10},{10,11},{12,13},{... | collective-permute-start | bytes 297224 | tf_op jit(solution)/shard_map/ppermute | solution.py:15
  92.1 9.1 %multiply_reduce_fusion.4 = f32[3,32,8,256]{3,2,1,0:T(8,128)} fusion(f32[6,3,3,32,8,256]{5,4,3,2,1,0:T(8,128)} %param.13, f32[6,3,32,8,256]{4,3,2,1,0:T(8,128)} %fusion.44), kind=kLoop, calls=%fused_computation.14 | loop fusion | flops 6881280 | bytes 19660800 | tf_op jit(solution)/shard_map/reduce_sum | solution.py:36
  109.5 5.4 collective-permute-done.8
  114.9 5.7 collective-permute-done.9
  121.5 7.6 %collective-permute-start.10 = (f32[3,32,1,258]{3,2,1,0:T(1,128)S(1)}, f32[3,32,1,258]{3,2,1,0:T(1,128)S(1)}, u32[]{:S(2)}, u32[]{:S(2)}) collective-permute-start(f32[3,32,1,258]{3,2,1,0:T(1,128)S(1)} %get-tuple-element.14), channel_id=1, source_target_pairs={{0,1},{1,2},{2,3},{4,5},{5,6},{6,7},{8,9},{9,10},{10,11},{12,13},{... | collective-permute-start | bytes 297224 | tf_op jit(solution)/shard_map/ppermute | solution.py:15
  139.4 9.1 %multiply_reduce_fusion.3 = f32[3,32,8,256]{3,2,1,0:T(8,128)} fusion(f32[6,3,3,32,8,256]{5,4,3,2,1,0:T(8,128)} %param.13, f32[6,3,32,8,256]{4,3,2,1,0:T(8,128)} %fusion.34), kind=kLoop, calls=%fused_computation.13 | loop fusion | flops 6881280 | bytes 19660800 | tf_op jit(solution)/shard_map/reduce_sum | solution.py:36
  156.9 5.4 collective-permute-done.12
  162.2 6.6 collective-permute-done.13
  169.7 6.7 collective-permute-start.14
  186.3 9.1 %multiply_reduce_fusion.2 = f32[3,32,8,256]{3,2,1,0:T(8,128)} fusion(f32[6,3,3,32,8,256]{5,4,3,2,1,0:T(8,128)} %param.13, f32[6,3,32,8,256]{4,3,2,1,0:T(8,128)} %fusion.24), kind=kLoop, calls=%fused_computation.12 | loop fusion | flops 6881280 | bytes 19660800 | tf_op jit(solution)/shard_map/reduce_sum | solution.py:36
  204.7 10.7 %gather_fusion = s32[1024]{0:T(1024)} fusion(s32[2048]{0:T(1024)S(1)} %copy-done, s32[1024]{0:T(1024)} %get-tuple-element.37), kind=kCustom, calls=%fused_computation | custom fusion | bytes 12288 | tf_op jit(solution)/shard_map/gather | solution.py:98
  219.2 5.8 collective-permute-start.18
  237.0 9.1 %multiply_reduce_fusion.1 = f32[3,32,8,256]{3,2,1,0:T(8,128)} fusion(f32[6,3,3,32,8,256]{5,4,3,2,1,0:T(8,128)} %param.13, f32[6,3,32,8,256]{4,3,2,1,0:T(8,128)} %fusion.14), kind=kLoop, calls=%fused_computation.11 | loop fusion | flops 6881280 | bytes 19660800 | tf_op jit(solution)/shard_map/reduce_sum | solution.py:36
  250.1 5.3 collective-permute-start.20
  265.1 17.6 %copy.28 = f32[3,32,8,256]{0,3,2,1:T(8,128)} copy(f32[3,32,8,256]{3,2,1,0:T(8,128)} %copy-done.7) | data formatting | bytes 1572864 | tf_op jit(solution)/shard_map/reduce_sum | solution.py:50
  282.7 16.7 %copy.27 = f32[3,32,8,256]{0,3,2,1:T(8,128)} copy(f32[3,32,8,256]{3,2,1,0:T(8,128)S(1)} %copy-done.14) | data formatting | bytes 1572864 | tf_op jit(solution)/shard_map/reduce_sum | solution.py:50
  299.3 17.5 %copy.26 = f32[3,32,8,256]{0,3,2,1:T(8,128)} copy(f32[3,32,8,256]{3,2,1,0:T(8,128)} %copy-done.15) | data formatting | bytes 1572864 | tf_op jit(solution)/shard_map/reduce_sum | solution.py:50
  334.4 9.2 %multiply_reduce_fusion = f32[3,32,8,256]{3,2,1,0:T(8,128)} fusion(f32[6,3,3,32,8,256]{5,4,3,2,1,0:T(8,128)} %param.13, f32[6,3,32,8,256]{4,3,2,1,0:T(8,128)} %fusion.4), kind=kLoop, calls=%fused_computation.10 | loop fusion | flops 6881280 | bytes 19660800 | tf_op jit(solution)/shard_map/reduce_sum | solution.py:36
  345.2 16.8 %copy.25 = f32[3,32,8,256]{0,3,2,1:T(8,128)} copy(f32[3,32,8,256]{3,2,1,0:T(8,128)S(1)} %multiply_reduce_fusion.6) | data formatting | bytes 1572864 | tf_op jit(solution)/shard_map/reduce_sum | solution.py:50
  362.0 52.0 %fusion.2 = f32[3,65536]{0,1:T(8,128)} fusion(f32[3,32,8,256]{0,3,2,1:T(8,128)} %copy.28, f32[3,32,8,256]{0,3,2,1:T(8,128)} %copy.27, f32[3,32,8,256]{0,3,2,1:T(8,128)} %copy.26, f32[3,32,8,256]{0,3,2,1:T(8,128)} %copy.25, pred[65536]{0:T(1024)(128)(4,1)S(1)} %copy-done.25, pred[65536]{0:T(1024)(128)(4,1)S(1)} %copy-done.24, ...), kind=kLoop, calls=%fused_computation.9 | loop fusion | flops 786432 | bytes 4194304 | tf_op jit(solution)/shard_map/jit(_where)/select_n | solution.py:95
  414.0 13.4 %gather_fusion.1 = f32[1024,3]{1,0:T(8,128)S(1)} fusion(f32[3,65536]{0,1:T(8,128)} %fusion.2, s32[1024]{0:T(1024)S(1)} %get-tuple-element.35), kind=kCustom, calls=%fused_computation.1 | custom fusion | bytes 28672 | tf_op jit(solution)/shard_map/gather | solution.py:97
  427.6 6.1 scatter_custom_fusion.1
  435.4 8.2 %scatter_custom_fusion = s32[2048]{0:T(1024)S(1)} fusion(s32[2048]{0:T(1024)S(1)} %compare_select_fusion, s32[2048]{0:T(1024)} %param.22, s32[]{:T(128)} %constant.14.clone.1), kind=kCustom, calls=%fused_computation.212 | custom fusion | bytes 8704 | tf_op jit(solution)/shard_map/scatter | solution.py:99
  443.7 135.1 %reduce-scatter.2.cloned.1.call-done = f32[64,16]{1,0:T(8,128)} async-done(((f32[2048,16]{1,0:T(8,128)}), f32[64,16]{1,0:T(8,128)}) %reduce-scatter.2.cloned.1.call-update) | async-done | bytes 4112 | tf_op jit(solution)/shard_map/reduce_scatter | solution.py:107
  580.4 37.2 %all-gather = f32[32,64,16]{1,2,0:T(8,128)S(1)} all-gather(f32[1,64,16]{1,2,0:T(8,128)S(1)} %copy.30), channel_id=1, replica_groups=mesh['gx'=8,'gy'=4] {'gx','gy'}, dimensions={0}, use_global_device_ids=true | all-gather | bytes 135168 | tf_op jit(solution)/shard_map/all_gather | solution.py:110
  618.2 6.2 gather_fusion.2
  624.7 27.0 %scatter_fusion = f32[3,65536]{0,1:T(8,128)} fusion(f32[3,65536]{0,1:T(8,128)} %fusion.2, s32[1024]{0:T(1024)S(1)} %get-tuple-element.36, f32[1024,3]{1,0:T(8,128)S(1)} %copy.32), kind=kCustom, calls=%fused_computation.5 | custom fusion | flops 3072 | bytes 40960 | tf_op jit(solution)/shard_map/scatter-add | solution.py:112
  651.7 19.5 %copy.33 = f32[3,32,8,256]{3,2,1,0:T(8,128)} copy(f32[3,32,8,256]{0,3,2,1:T(8,128)} %bitcast.174) | data formatting | bytes 1572864 | tf_op jit(solution)/shard_map/reshape | solution.py:113
  (198 shorter events, 142.6 us)
Async XLA Ops:
  6.5 572.3 %reduce-scatter.2.cloned.1.call-start = ((), (), s32[]{:S(2)}) async-start(), calls=%async_computation.1 | async-start | bytes 1081344 | tf_op jit(solution)/shard_map/reduce_scatter | solution.py:107
  7.6 140.8 %copy-start.19 = (pred[32,8,256]{2,1,0:T(8,128)(4,1)}, pred[32,8,256]{2,1,0:T(8,128)(4,1)S(1)}, u32[]{:S(2)}) copy-start(pred[32,8,256]{2,1,0:T(8,128)(4,1)S(1)} %get-tuple-element.33) | copy-start | bytes 196612
  7.6 140.8 %copy-start.21 = (pred[32,8,256]{2,1,0:T(8,128)(4,1)}, pred[32,8,256]{2,1,0:T(8,128)(4,1)S(1)}, u32[]{:S(2)}) copy-start(pred[32,8,256]{2,1,0:T(8,128)(4,1)S(1)} %get-tuple-element.32) | copy-start | bytes 196612
  7.6 189.5 %copy-start.17 = (pred[32,8,256]{2,1,0:T(8,128)(4,1)}, pred[32,8,256]{2,1,0:T(8,128)(4,1)S(1)}, u32[]{:S(2)}) copy-start(pred[32,8,256]{2,1,0:T(8,128)(4,1)S(1)} %get-tuple-element.31) | copy-start | bytes 196612
  7.7 189.5 %copy-start.18 = (pred[32,8,256]{2,1,0:T(8,128)(4,1)}, pred[32,8,256]{2,1,0:T(8,128)(4,1)S(1)}, u32[]{:S(2)}) copy-start(pred[32,8,256]{2,1,0:T(8,128)(4,1)S(1)} %get-tuple-element.34) | copy-start | bytes 196612
  10.8 21.6 %collective-permute-start = (f32[3,32,8,1]{3,2,1,0:T(8,128)S(1)}, f32[3,32,8,1]{3,2,1,0:T(8,128)S(1)}, u32[]{:S(2)}, u32[]{:S(2)}) collective-permute-start(f32[3,32,8,1]{3,2,1,0:T(8,128)S(1)} %get-tuple-element.30), channel_id=1, source_target_pairs={{0,4},{4,8},{8,12},{12,16},{16,20},{20,24},{24,28},{1,5},{5,9},{9,... | collective-permute-start | bytes 9224 | tf_op jit(solution)/shard_map/ppermute | solution.py:15
  15.6 16.8 %collective-permute-start.1 = (f32[3,32,8,1]{3,2,1,0:T(8,128)S(1)}, f32[3,32,8,1]{3,2,1,0:T(8,128)S(1)}, u32[]{:S(2)}, u32[]{:S(2)}) collective-permute-start(f32[3,32,8,1]{3,2,1,0:T(8,128)S(1)} %get-tuple-element.29), channel_id=1, source_target_pairs={{4,0},{8,4},{12,8},{16,12},{20,16},{24,20},{28,24},{5,1},{9,5},{13... | collective-permute-start | bytes 9224 | tf_op jit(solution)/shard_map/ppermute | solution.py:17
  33.3 5.1 collective-permute-start.2
  34.6 5.0 collective-permute-start.3
  55.9 11.1 %collective-permute-start.4 = (f32[3,32,8,1]{3,2,1,0:T(8,128)S(1)}, f32[3,32,8,1]{3,2,1,0:T(8,128)S(1)}, u32[]{:S(2)}, u32[]{:S(2)}) collective-permute-start(f32[3,32,8,1]{3,2,1,0:T(8,128)S(1)} %get-tuple-element.28), channel_id=1, source_target_pairs={{0,4},{4,8},{8,12},{12,16},{16,20},{20,24},{24,28},{1,5},{5,9},{9,... | collective-permute-start | bytes 9224 | tf_op jit(solution)/shard_map/ppermute | solution.py:15
  60.3 12.8 %collective-permute-start.5 = (f32[3,32,8,1]{3,2,1,0:T(8,128)S(1)}, f32[3,32,8,1]{3,2,1,0:T(8,128)S(1)}, u32[]{:S(2)}, u32[]{:S(2)}) collective-permute-start(f32[3,32,8,1]{3,2,1,0:T(8,128)S(1)} %get-tuple-element.27), channel_id=1, source_target_pairs={{4,0},{8,4},{12,8},{16,12},{20,16},{24,20},{28,24},{5,1},{9,5},{13... | collective-permute-start | bytes 9224 | tf_op jit(solution)/shard_map/ppermute | solution.py:17
  73.9 11.4 %collective-permute-start.6 = (f32[3,32,1,258]{3,2,1,0:T(1,128)S(1)}, f32[3,32,1,258]{3,2,1,0:T(1,128)S(1)}, u32[]{:S(2)}, u32[]{:S(2)}) collective-permute-start(f32[3,32,1,258]{3,2,1,0:T(1,128)S(1)} %get-tuple-element.16), channel_id=1, source_target_pairs={{0,1},{1,2},{2,3},{4,5},{5,6},{6,7},{8,9},{9,10},{10,11},{12,13},{... | collective-permute-start | bytes 297224 | tf_op jit(solution)/shard_map/ppermute | solution.py:15
  81.1 5.0 collective-permute-start.7
  103.8 11.1 %collective-permute-start.8 = (f32[3,32,8,1]{3,2,1,0:T(8,128)S(1)}, f32[3,32,8,1]{3,2,1,0:T(8,128)S(1)}, u32[]{:S(2)}, u32[]{:S(2)}) collective-permute-start(f32[3,32,8,1]{3,2,1,0:T(8,128)S(1)} %get-tuple-element.26), channel_id=1, source_target_pairs={{0,4},{4,8},{8,12},{12,16},{16,20},{20,24},{24,28},{1,5},{5,9},{9,... | collective-permute-start | bytes 9224 | tf_op jit(solution)/shard_map/ppermute | solution.py:15
  108.2 12.4 %collective-permute-start.9 = (f32[3,32,8,1]{3,2,1,0:T(8,128)S(1)}, f32[3,32,8,1]{3,2,1,0:T(8,128)S(1)}, u32[]{:S(2)}, u32[]{:S(2)}) collective-permute-start(f32[3,32,8,1]{3,2,1,0:T(8,128)S(1)} %get-tuple-element.25), channel_id=1, source_target_pairs={{4,0},{8,4},{12,8},{16,12},{20,16},{24,20},{28,24},{5,1},{9,5},{13... | collective-permute-start | bytes 9224 | tf_op jit(solution)/shard_map/ppermute | solution.py:17
  121.5 11.5 %collective-permute-start.10 = (f32[3,32,1,258]{3,2,1,0:T(1,128)S(1)}, f32[3,32,1,258]{3,2,1,0:T(1,128)S(1)}, u32[]{:S(2)}, u32[]{:S(2)}) collective-permute-start(f32[3,32,1,258]{3,2,1,0:T(1,128)S(1)} %get-tuple-element.14), channel_id=1, source_target_pairs={{0,1},{1,2},{2,3},{4,5},{5,6},{6,7},{8,9},{9,10},{10,11},{12,13},{... | collective-permute-start | bytes 297224 | tf_op jit(solution)/shard_map/ppermute | solution.py:15
  129.1 4.3 collective-permute-start.11
  151.1 11.1 %collective-permute-start.12 = (f32[3,32,8,1]{3,2,1,0:T(8,128)S(1)}, f32[3,32,8,1]{3,2,1,0:T(8,128)S(1)}, u32[]{:S(2)}, u32[]{:S(2)}) collective-permute-start(f32[3,32,8,1]{3,2,1,0:T(8,128)S(1)} %get-tuple-element.24), channel_id=1, source_target_pairs={{0,4},{4,8},{8,12},{12,16},{16,20},{20,24},{24,28},{1,5},{5,9},{9,... | collective-permute-start | bytes 9224 | tf_op jit(solution)/shard_map/ppermute | solution.py:15
  155.6 13.3 %collective-permute-start.13 = (f32[3,32,8,1]{3,2,1,0:T(8,128)S(1)}, f32[3,32,8,1]{3,2,1,0:T(8,128)S(1)}, u32[]{:S(2)}, u32[]{:S(2)}) collective-permute-start(f32[3,32,8,1]{3,2,1,0:T(8,128)S(1)} %get-tuple-element.23), channel_id=1, source_target_pairs={{4,0},{8,4},{12,8},{16,12},{20,16},{24,20},{28,24},{5,1},{9,5},{13... | collective-permute-start | bytes 9224 | tf_op jit(solution)/shard_map/ppermute | solution.py:17
  169.7 10.6 %collective-permute-start.14 = (f32[3,32,1,258]{3,2,1,0:T(1,128)S(1)}, f32[3,32,1,258]{3,2,1,0:T(1,128)S(1)}, u32[]{:S(2)}, u32[]{:S(2)}) collective-permute-start(f32[3,32,1,258]{3,2,1,0:T(1,128)S(1)} %get-tuple-element.12), channel_id=1, source_target_pairs={{0,1},{1,2},{2,3},{4,5},{5,6},{6,7},{8,9},{9,10},{10,11},{12,13},{... | collective-permute-start | bytes 297224 | tf_op jit(solution)/shard_map/ppermute | solution.py:15
  176.4 4.0 collective-permute-start.15
  198.3 17.0 %collective-permute-start.16 = (f32[3,32,8,1]{3,2,1,0:T(8,128)}, f32[3,32,8,1]{3,2,1,0:T(8,128)S(1)}, u32[]{:S(2)}, u32[]{:S(2)}) collective-permute-start(f32[3,32,8,1]{3,2,1,0:T(8,128)} %get-tuple-element.22), channel_id=1, source_target_pairs={{0,4},{4,8},{8,12},{12,16},{16,20},{20,24},{24,28},{1,5},{5,9},{9,... | collective-permute-start | bytes 9224 | tf_op jit(solution)/shard_map/ppermute | solution.py:15
  202.7 14.5 %collective-permute-start.17 = (f32[3,32,8,1]{3,2,1,0:T(8,128)}, f32[3,32,8,1]{3,2,1,0:T(8,128)}, u32[]{:S(2)}, u32[]{:S(2)}) collective-permute-start(f32[3,32,8,1]{3,2,1,0:T(8,128)} %get-tuple-element.21), channel_id=1, source_target_pairs={{4,0},{8,4},{12,8},{16,12},{20,16},{24,20},{28,24},{5,1},{9,5},{13... | collective-permute-start | bytes 9224 | tf_op jit(solution)/shard_map/ppermute | solution.py:17
  219.2 10.8 %collective-permute-start.18 = (f32[3,32,1,258]{3,2,1,0:T(1,128)S(1)}, f32[3,32,1,258]{3,2,1,0:T(1,128)S(1)}, u32[]{:S(2)}, u32[]{:S(2)}) collective-permute-start(f32[3,32,1,258]{3,2,1,0:T(1,128)S(1)} %get-tuple-element.10), channel_id=1, source_target_pairs={{0,1},{1,2},{2,3},{4,5},{5,6},{6,7},{8,9},{9,10},{10,11},{12,13},{... | collective-permute-start | bytes 297224 | tf_op jit(solution)/shard_map/ppermute | solution.py:15
  225.0 5.0 collective-permute-start.19
  250.1 66.8 %collective-permute-start.20 = (f32[3,32,8,1]{3,2,1,0:T(8,128)}, f32[3,32,8,1]{3,2,1,0:T(8,128)S(1)}, u32[]{:S(2)}, u32[]{:S(2)}) collective-permute-start(f32[3,32,8,1]{3,2,1,0:T(8,128)} %get-tuple-element.20), channel_id=1, source_target_pairs={{0,4},{4,8},{8,12},{12,16},{16,20},{20,24},{24,28},{1,5},{5,9},{9,... | collective-permute-start | bytes 9224 | tf_op jit(solution)/shard_map/ppermute | solution.py:15
  255.4 61.5 %collective-permute-start.21 = (f32[3,32,8,1]{3,2,1,0:T(8,128)}, f32[3,32,8,1]{3,2,1,0:T(8,128)}, u32[]{:S(2)}, u32[]{:S(2)}) collective-permute-start(f32[3,32,8,1]{3,2,1,0:T(8,128)} %get-tuple-element.19), channel_id=1, source_target_pairs={{4,0},{8,4},{12,8},{16,12},{20,16},{24,20},{28,24},{5,1},{9,5},{13... | collective-permute-start | bytes 9224 | tf_op jit(solution)/shard_map/ppermute | solution.py:17
  318.9 8.5 %collective-permute-start.22 = (f32[3,32,1,258]{3,2,1,0:T(1,128)S(1)}, f32[3,32,1,258]{3,2,1,0:T(1,128)S(1)}, u32[]{:S(2)}, u32[]{:S(2)}) collective-permute-start(f32[3,32,1,258]{3,2,1,0:T(1,128)S(1)} %get-tuple-element.8), channel_id=1, source_target_pairs={{0,1},{1,2},{2,3},{4,5},{5,6},{6,7},{8,9},{9,10},{10,11},{12,13},{... | collective-permute-start | bytes 297224 | tf_op jit(solution)/shard_map/ppermute | solution.py:15
  322.2 5.2 collective-permute-start.23
  362.0 73.1 %copy-start.26 = (f32[64,16,16]{0,2,1:T(8,128)S(1)}, f32[64,16,16]{0,2,1:T(8,128)}, u32[]{:S(2)}) copy-start(f32[64,16,16]{0,2,1:T(8,128)} %param.23) | copy-start | bytes 196612
  414.0 204.2 %copy-start.28 = (s32[1024]{0:T(1024)S(1)}, s32[1024]{0:T(1024)}, u32[]{:S(2)}) copy-start(s32[1024]{0:T(1024)} %get-tuple-element.5) | copy-start | bytes 12292
  435.0 189.4 %copy-start.27 = (f32[3,1024]{1,0:T(4,128)S(1)}, f32[3,1024]{1,0:T(4,128)}, u32[]{:S(2)}) copy-start(f32[3,1024]{1,0:T(4,128)} %param.20) | copy-start | bytes 36868
  (26 other events, 331.9 us)
Sparse Core Ops, SparseCore 0:
  435.2 143.6 reduce-scatter.1
where the time goes:
time: 687 us; the launch traced here: 678 us
  other arithmetic  205 us (30%)
  waiting for transfers between devices  188 us (27%)
  local copies, waits for them, and re-layouts  156 us (23%)
  starting transfers between devices  76.7 us (11%)
  blocking collectives  37.2 us (5%)
  between operations  14.3 us (2%)
    reduce_scatter x1, waiting for transfers between devices, shards(): lax.psum_scatter(local_totals, ('gx', 'gy'), scatter_dimension=0, tiled=T...  135 us
    reduce_sum x4, local copies, waits for them, and re-layouts, pivot(): return jnp.sum(pivot_inverses * field[None], axis=1)  68.5 us
    ppermute x12, starting transfers between devices, padded_2(): lax.ppermute(tail, axis, [(i, (i + 1) % count) for i in range(ends)])  59.5 us
    reduce_sum x6, other arithmetic, gather_beside(): return jnp.sum(couplings * beside[:, None], axis=(0, 2))  54.9 us
    select_n x4, other arithmetic, shards(): sweep_field = jnp.where(chosen, current, sweep_field)  52.3 us
    all_gather x1, blocking collectives, shards(): values_all = lax.all_gather(own_values, ('gx', 'gy'), axis=0, tiled=True)  37.2 us
    unnamed x25, other arithmetic  32 us
    ppermute x12, waiting for transfers between devices, padded_2(): lax.ppermute(tail, axis, [(i, (i + 1) % count) for i in range(ends)])  31.6 us
  transfers between devices with their start and end apart: 25, of which 11 were waited for; matrix products, arithmetic and copies ran while one was open for 14% of the time, Pallas kernels for 0%

commit v1 on v0

v1 whole, which is shorter than its diff:
```python
import functools

import jax
import jax.numpy as jnp
from jax import lax
from jax.experimental import pallas as pl
from jax.experimental.pallas import tpu as pltpu
from jax.sharding import PartitionSpec as P

MESH = pl.DeviceIdType.MESH
LANES = 128
F32 = jnp.float32
BF16 = jnp.bfloat16


def shift_of(n):
    assert n & (n - 1) == 0
    return n.bit_length() - 1


def parts_of(x, count=3):
    parts = []
    for k in range(count):
        part = x.astype(BF16)
        parts.append(part)
        if k + 1 < count:
            x = x - part.astype(F32)
    return parts


def dot_nn(a, b):
    return lax.dot_general(a, b, (((1,), (0,)), ((), ())), preferred_element_type=F32)


def dot_nt(a, b):
    return lax.dot_general(a, b, (((1,), (1,)), ((), ())), preferred_element_type=F32)


def dot_exact(a, b):
    return lax.dot_general(
        a, b, (((1,), (0,)), ((), ())), precision=lax.Precision.HIGHEST, preferred_element_type=F32
    )


def one_hot(row, count):
    index = lax.broadcasted_iota(jnp.int32, (count, row.shape[1]), 0)
    return jnp.where(index == row, 1.0, 0.0).astype(BF16)


def kernel(
    gx,
    gy,
    rhs,
    couplings,
    pivots,
    colours,
    cells,
    wells,
    segs,
    gather,
    ret,
    slots,
    counts,
    inverses,
    out,
    coup,
    fld,
    upper,
    acc,
    cx_edge,
    cy_edge,
    x_add,
    y_add,
    xsend,
    ysend,
    xhalo,
    yhalo,
    hot_x,
    hot_r,
    hot_hi,
    hot_lo,
    totals,
    got_a,
    sum_a,
    got_b,
    values,
    load_sem,
    halo_send,
    halo_recv,
    a_send,
    a_recv,
    b_send,
    b_recv,
    c_send,
    c_recv,
    d_send,
    d_recv,
):
    _, nz, cy, cx = rhs.shape
    owned, seg, _ = inverses.shape
    ix = lax.axis_index("gx")
    iy = lax.axis_index("gy")

    loads = [
        pltpu.make_async_copy(couplings.at[k], coup.at[k], load_sem.at[k]) for k in range(6)
    ]
    for load in loads:
        load.start()

    @pl.when(ix == 0)
    def _():
        xhalo[:, 0] = jnp.zeros_like(xhalo[:, 0])

    @pl.when(ix == gx - 1)
    def _():
        xhalo[:, 1] = jnp.zeros_like(xhalo[:, 1])

    @pl.when(iy == 0)
    def _():
        yhalo[:, 0] = jnp.zeros_like(yhalo[:, 0])

    @pl.when(iy == gy - 1)
    def _():
        yhalo[:, 1] = jnp.zeros_like(yhalo[:, 1])

    barrier = pltpu.get_barrier_semaphore()
    for d in range(1, gx):
        pl.semaphore_signal(
            barrier, inc=1, device_id=(lax.rem(ix + d, gx), iy), device_id_type=MESH
        )
    for d in range(1, gy):
        pl.semaphore_signal(
            barrier, inc=1, device_id=(ix, lax.rem(iy + d, gy)), device_id_type=MESH
        )

    lane = lax.broadcasted_iota(jnp.int32, (cy, LANES), 1)
    wide_lane = lax.broadcasted_iota(jnp.int32, (cy, cx), 1)
    row = lax.broadcasted_iota(jnp.int32, (cy, cx), 0)
    tiles = cx // LANES

    for u in range(3):
        fld[u, 0] = jnp.zeros((cy, cx), F32)
        fld[u, nz + 1] = jnp.zeros((cy, cx), F32)

    def pivoted(z, field):
        return [
            pivots[i, 0, z] * field[0] + pivots[i, 1, z] * field[1] + pivots[i, 2, z] * field[2]
            for i in range(3)
        ]

    def emit(slot, z, new, packs):
        result = []
        for j in range(3):
            ysend[slot, 0, j, pl.ds(z, 1), :] = new[j][cy - 1 : cy]
            ysend[slot, 1, j, pl.ds(z, 1), :] = new[j][0:1]
        for j in range(3):
            moved = pltpu.roll(new[j][:, cx - LANES :], z + 1, 1)
            result.append(jnp.where(lane == z, moved, packs[j]))
        for j in range(3):
            moved = pltpu.roll(new[j][:, :LANES], z, 1)
            result.append(jnp.where(lane == z, moved, packs[3 + j]))
        return tuple(result)

    no_packs = tuple(jnp.zeros((cy, LANES), F32) for _ in range(6))

    def halo_copies(slot):
        found = []
        for side, (buffers, there, inside) in enumerate(
            (
                ((xsend, xhalo), (ix + 1, iy), ix < gx - 1),
                ((xsend, xhalo), (ix - 1, iy), ix > 0),
                ((ysend, yhalo), (ix, iy + 1), iy < gy - 1),
                ((ysend, yhalo), (ix, iy - 1), iy > 0),
            )
        ):
            copy = pltpu.make_async_remote_copy(
                src_ref=buffers[0].at[slot, side % 2],
                dst_ref=buffers[1].at[slot, side % 2],
                send_sem=halo_send.at[slot, side],
                recv_sem=halo_recv.at[slot, side],
                device_id=there,
                device_id_type=MESH,
            )
            found.append((copy, inside))
        return found

    def send_halo(slot, packs):
        for j in range(3):
            xsend[slot, 0, j] = packs[j]
            xsend[slot, 1, j] = packs[3 + j]
        for copy, inside in halo_copies(slot):
            pl.when(inside)(copy.start)

    def take_halo(slot):
        copies = halo_copies(slot)
        for side in range(4):
            pl.when(copies[side ^ 1][1])(copies[side][0].wait_recv)
        for side in range(2):
            for i in range(3):
                x_add[side, i] = sum(cx_edge[side, i, j] * xhalo[slot, side, j] for j in range(3))
                y_add[side, i] = sum(cy_edge[side, i, j] * yhalo[slot, side, j] for j in range(3))

    def interior(base):
        def step(z, carry):
            total = [base[i, z] for i in range(3)]
            for j in range(3):
                here = fld[j, z + 1]
                beside = (
                    jnp.where(wide_lane == 0, 0.0, pltpu.roll(here, 1, 1)),
                    jnp.where(wide_lane == cx - 1, 0.0, pltpu.roll(here, cx - 1, 1)),
                    jnp.where(row == 0, 0.0, pltpu.roll(here, 1, 0)),
                    jnp.where(row == cy - 1, 0.0, pltpu.roll(here, cy - 1, 0)),
                    fld[j, z],
                    fld[j, z + 2],
                )
                for i in range(3):
                    for k in range(6):
                        total[i] = total[i] - coup[k, i, j, z] * beside[k]
            for i in range(3):
                acc[i, z] = total[i]
            return carry

        lax.fori_loop(0, nz, step, 0, unroll=2)

    def finish(colour, slot, forward):
        def step(z, packs):
            current = []
            for i in range(3):
                first = jnp.where(lane == 0, pltpu.roll(x_add[0, i], LANES - z, 1), 0.0)
                last = jnp.where(lane == LANES - 1, pltpu.roll(x_add[1, i], LANES - 1 - z, 1), 0.0)
                pieces = [jnp.zeros((cy, LANES), F32)] * tiles
                pieces[0] = pieces[0] + first
                pieces[-1] = pieces[-1] + last
                along_x = jnp.concatenate(pieces, axis=1) if tiles > 1 else pieces[0]
                along_y = jnp.where(row == 0, y_add[0, i, pl.ds(z, 1), :], 0.0) + jnp.where(
                    row == cy - 1, y_add[1, i, pl.ds(z, 1), :], 0.0
                )
                current.append(acc[i, z] - along_x - along_y)
            chosen = colours[z] == colour
            new = pivoted(z, current)
            for i in range(3):
                if forward:
                    upper[i, z] = jnp.where(chosen, current[i], upper[i, z])
                before = 0.0 if forward and colour == 3 else fld[i, z + 1]
                new[i] = jnp.where(chosen, new[i], before)
                fld[i, z + 1] = new[i]
            if slot is None:
                return packs
            return emit(slot, z, new, packs)

        packs = lax.fori_loop(0, nz, step, no_packs, unroll=2)
        if slot is not None:
            send_halo(slot, packs)

    def first(z, packs):
        chosen = colours[z] == 0
        field = [rhs[i, z] for i in range(3)]
        new = pivoted(z, field)
        for i in range(3):
            upper[i, z] = field[i]
            new[i] = jnp.where(chosen, new[i], 0.0)
            fld[i, z + 1] = new[i]
        return emit(0, z, new, packs)

    packs = lax.fori_loop(0, nz, first, no_packs, unroll=2)
    pl.semaphore_wait(barrier, gx + gy - 2)
    send_halo(0, packs)

    cell = cells[...]
    hot_x[...] = one_hot(cell & (cx - 1), cx)
    hot_r[...] = one_hot(cell >> shift_of(cx), nz * cy)
    per_owner = owned * seg // LANES
    key = wells[...] * seg + segs[...]
    high = key >> shift_of(LANES)
    owner = high >> shift_of(per_owner)
    placed = (owner & (gy - 1)) * gx + (owner >> shift_of(gy))
    high = placed * per_owner + (high & (per_owner - 1))
    hot_hi[...] = one_hot(high, gx * gy * per_owner)
    hot_lo[...] = one_hot(key & (LANES - 1), LANES)

    for load in loads:
        load.wait()

    for i in range(3):
        for j in range(3):

            def pack(z, carry):
                left, right = carry
                moved = pltpu.roll(coup[0, i, j, z][:, :LANES], z, 1)
                left = jnp.where(lane == z, moved, left)
                moved = pltpu.roll(coup[1, i, j, z][:, cx - LANES :], z + 1, 1)
                right = jnp.where(lane == z, moved, right)
                cy_edge[0, i, j, pl.ds(z, 1), :] = coup[2, i, j, z, 0:1, :]
                cy_edge[1, i, j, pl.ds(z, 1), :] = coup[3, i, j, z, cy - 1 : cy, :]
                return left, right

            left, right = lax.fori_loop(0, nz, pack, no_packs[:2], unroll=4)
            cx_edge[0, i, j] = left
            cx_edge[1, i, j] = right

    slot = 0
    for colour in (1, 2, 3):
        interior(rhs)
        take_halo(slot)
        slot += 1
        finish(colour, slot, True)
    for colour in (2, 1, 0):
        interior(upper)
        take_halo(slot)
        slot += 1
        finish(colour, slot if colour > 0 else None, False)

    term = jnp.zeros(hot_r.shape, F32)
    for u in range(3):
        field = fld[u, 1 : nz + 1].reshape(nz * cy, cx)
        read = sum(dot_nn(part, hot_x[...]) for part in parts_of(field))
        term = term + read * gather[u : u + 1, :]
    term = jnp.sum(term * hot_r[...].astype(F32), axis=0, keepdims=True)
    spread = hot_lo[...].astype(F32) * term
    sums = sum(dot_nt(hot_hi[...], part) for part in parts_of(spread))
    totals[...] = sums.reshape(totals.shape)

    def along_gy(src, dst, send, recv, d):
        return pltpu.make_async_remote_copy(
            src_ref=src,
            dst_ref=dst,
            send_sem=send.at[d],
            recv_sem=recv.at[d],
            device_id=(ix, lax.rem(iy + d, gy)),
            device_id_type=MESH,
        )

    def along_gx(src, dst, send, recv, d):
        return pltpu.make_async_remote_copy(
            src_ref=src,
            dst_ref=dst,
            send_sem=send.at[d],
            recv_sem=recv.at[d],
            device_id=(lax.rem(ix + d, gx), iy),
            device_id_type=MESH,
        )

    copies_a = [
        along_gy(totals.at[lax.rem(iy + d, gy)], got_a.at[d], a_send, a_recv, d)
        for d in range(1, gy)
    ]
    for copy in copies_a:
        copy.start()

    first_well = (ix * gy + iy) * owned
    at_row = lax.div(first_well, LANES)
    at_lane = lax.rem(first_well, LANES)

    def own_row(table):
        line = jnp.broadcast_to(table[pl.ds(at_row, 1), :], (8, LANES))
        return pltpu.roll(line, LANES - at_lane, 1)[0:1, :owned]

    slot_row = own_row(slots) - first_well
    count_row = own_row(counts)
    by_slot = lax.broadcasted_iota(jnp.int32, (owned, owned), 0)
    by_well = lax.broadcasted_iota(jnp.int32, (owned, owned), 1)
    order = jnp.where(slot_row == by_slot, 1.0, 0.0)
    live = jnp.sum(jnp.where(slot_row == by_slot, count_row, 0), axis=1, keepdims=True)
    slot_column = jnp.sum(jnp.where(by_slot == by_well, slot_row, 0), axis=1, keepdims=True)
    back_index = lax.broadcasted_iota(jnp.int32, (owned, owned * seg), 1) >> shift_of(seg)
    back = jnp.where(back_index == slot_column, 1.0, 0.0)
    wells_row = LANES // seg
    lane_of = lax.broadcasted_iota(jnp.int32, (owned, LANES), 1)
    well_of = lax.broadcasted_iota(jnp.int32, (owned, LANES), 0)
    mine = (lane_of >> shift_of(seg)) == (well_of & (wells_row - 1))
    fold_from = lax.broadcasted_iota(jnp.int32, (LANES, seg), 0)
    fold_to = lax.broadcasted_iota(jnp.int32, (LANES, seg), 1)
    fold = jnp.where((fold_from & (seg - 1)) == fold_to, 1.0, 0.0)
    segment = lax.broadcasted_iota(jnp.int32, (owned, seg), 1)

    for copy in copies_a:
        copy.wait_recv()
    summed = totals[iy]
    for d in range(1, gy):
        summed = summed + got_a[d]
    sum_a[...] = summed
    copies_b = [
        along_gx(sum_a.at[lax.rem(ix + d, gx)], got_b.at[d], b_send, b_recv, d)
        for d in range(1, gx)
    ]
    for copy in copies_b:
        copy.start()
    for copy in copies_b:
        copy.wait_recv()
    own = sum_a[ix]
    for d in range(1, gx):
        own = own + got_b[d]

    rows = jnp.broadcast_to(own[:, None, :], (per_owner, wells_row, LANES)).reshape(owned, LANES)
    by_segment = dot_exact(dot_exact(order, jnp.where(mine, rows, 0.0)), fold)
    by_segment = jnp.where(segment < live, by_segment, 0.0)
    solved = jnp.sum(inverses[...] * by_segment[:, None, :], axis=2, keepdims=True)
    inner = lax.broadcasted_iota(jnp.int32, (owned, seg, LANES), 1)
    outer = lax.broadcasted_iota(jnp.int32, (owned, seg, LANES), 2) & (seg - 1)
    alive = (inner == outer) & (inner < live[:, :, None])
    solved = jnp.where(alive, solved, 0.0).reshape(owned * seg, LANES)
    spread_back = jnp.where(mine, dot_exact(back, solved), 0.0)
    values[iy, ix] = jnp.sum(spread_back.reshape(per_owner, wells_row, LANES), axis=1)

    def sent_c(d):
        return along_gx(values.at[iy, ix], values.at[iy, ix], c_send, c_recv, d)

    def due_c(d):
        there = lax.rem(ix + gx - d, gx)
        return along_gx(values.at[iy, there], values.at[iy, there], c_send, c_recv, d)

    for d in range(1, gx):
        sent_c(d).start()
    for d in range(1, gx):
        due_c(d).wait_recv()

    def sent_d(d):
        return along_gy(values.at[iy], values.at[iy], d_send, d_recv, d)

    def due_d(d):
        there = lax.rem(iy + gy - d, gy)
        return along_gy(values.at[there], values.at[there], d_send, d_recv, d)

    for d in range(1, gy):
        sent_d(d).start()
    for d in range(1, gy):
        due_d(d).wait_recv()

    table = values[...].reshape(gx * gy * per_owner, LANES)
    read = sum(dot_nn(part, hot_lo[...]) for part in parts_of(table))
    at_perfs = jnp.sum(read * hot_hi[...].astype(F32), axis=0, keepdims=True)
    for u in range(3):
        weights = hot_x[...].astype(F32) * (ret[u : u + 1, :] * at_perfs)
        change = sum(dot_nt(hot_r[...], part) for part in parts_of(weights))
        out[u] = fld[u, 1 : nz + 1] - change.reshape(nz, cy, cx)

    for done in range(slot):
        for copy, inside in halo_copies(done):
            pl.when(inside)(copy.wait_send)
    for copy in copies_a + copies_b:
        copy.wait_send()
    for d in range(1, gx):
        sent_c(d).wait_send()
    for d in range(1, gy):
        sent_d(d).wait_send()


def shards(
    gx,
    gy,
    rhs_field,
    couplings,
    pivot_inverses,
    colours,
    perf_cells,
    perf_wells,
    perf_segments,
    perf_gather,
    perf_return,
    well_slot,
    seg_count,
    well_inverses,
):
    _, nz, cy, cx = rhs_field.shape
    owned, seg, _ = well_inverses.shape
    perfs = perf_cells.shape[0]
    per_owner = owned * seg // LANES
    high = gx * gy * per_owner
    vmem = pl.BlockSpec(memory_space=pltpu.VMEM)
    dma = pltpu.SemaphoreType.DMA
    return pl.pallas_call(
        functools.partial(kernel, gx, gy),
        out_shape=jax.ShapeDtypeStruct(rhs_field.shape, F32),
        in_specs=[vmem, pl.BlockSpec(memory_space=pl.ANY)] + [vmem] * 10,
        out_specs=vmem,
        scratch_shapes=[
            pltpu.VMEM(couplings.shape, F32),
            pltpu.VMEM((3, nz + 2, cy, cx), F32),
            pltpu.VMEM((3, nz, cy, cx), F32),
            pltpu.VMEM((3, nz, cy, cx), F32),
            pltpu.VMEM((2, 3, 3, cy, LANES), F32),
            pltpu.VMEM((2, 3, 3, nz, cx), F32),
            pltpu.VMEM((2, 3, cy, LANES), F32),
            pltpu.VMEM((2, 3, nz, cx), F32),
            pltpu.VMEM((6, 2, 3, cy, LANES), F32),
            pltpu.VMEM((6, 2, 3, nz, cx), F32),
            pltpu.VMEM((6, 2, 3, cy, LANES), F32),
            pltpu.VMEM((6, 2, 3, nz, cx), F32),
            pltpu.VMEM((cx, perfs), BF16),
            pltpu.VMEM((nz * cy, perfs), BF16),
            pltpu.VMEM((high, perfs), BF16),
            pltpu.VMEM((LANES, perfs), BF16),
            pltpu.VMEM((gy, gx, per_owner, LANES), F32),
            pltpu.VMEM((gy, gx, per_owner, LANES), F32),
            pltpu.VMEM((gx, per_owner, LANES), F32),
            pltpu.VMEM((gx, per_owner, LANES), F32),
            pltpu.VMEM((gy, gx, per_owner, LANES), F32),
            dma((6,)),
            dma((6, 4)),
            dma((6, 4)),
            dma((gy,)),
            dma((gy,)),
            dma((gx,)),
            dma((gx,)),
            dma((gx,)),
            dma((gx,)),
            dma((gy,)),
            dma((gy,)),
        ],
        compiler_params=pltpu.CompilerParams(
            collective_id=0, has_side_effects=True, vmem_limit_bytes=52 * 2**20
        ),
        name="precondition",
    )(
        rhs_field,
        couplings,
        pivot_inverses,
        colours,
        perf_cells.reshape(1, perfs),
        perf_wells.reshape(1, perfs),
        perf_segments.reshape(1, perfs),
        perf_gather,
        perf_return,
        well_slot.reshape(-1, LANES),
        seg_count.reshape(-1, LANES),
        well_inverses,
    )


def solution(mesh):
    return jax.shard_map(
        functools.partial(shards, mesh.shape["gx"], mesh.shape["gy"]),
        mesh=mesh,
        in_specs=(
            P(None, None, "gy", "gx"),
            P(None, None, None, None, "gy", "gx"),
            P(None, None, None, "gy", "gx"),
            P(None, "gy", "gx"),
            P(("gx", "gy")),
            P(("gx", "gy")),
            P(("gx", "gy")),
            P(None, ("gx", "gy")),
            P(None, ("gx", "gy")),
            P(),
            P(),
            P(("gx", "gy"), None, None),
        ),
        out_specs=P(None, None, "gy", "gx"),
        check_vma=False,
    )
```

time: 687 us -> 77.3 us (0.11); the launches traced: 678 us -> 76.7 us
  other arithmetic: 205 us -> 0 us
  waiting for transfers between devices: 188 us -> 0 us
  local copies, waits for them, and re-layouts: 156 us -> 7.89 us
  starting transfers between devices: 76.7 us -> 0 us
  Pallas kernels: 0 us -> 68.8 us
  blocking collectives: 37.2 us -> 0 us
  between operations: 14.3 us -> 0.03 us
    reduce_scatter x1 -> x0, waiting for transfers between devices: 135 us -> none  [shards(): lax.psum_scatter(local_totals, ('gx', 'gy'), scatter_dimension=0, tiled=T...]
    ppermute x24 -> x0, starting transfers between devices: 76.7 us -> none  [the longest x12 59.5 us: padded_2(): lax.ppermute(tail, axis, [(i, (i + 1) % count) for i in range(ends)])]
    pallas_call x0 -> x1, Pallas kernels: none -> 68.8 us  [shards(): pl.pallas_call(functools.partial(kernel, gx, gy), out_shape=jax.ShapeDtyp...]
    reduce_sum x4 -> x0, local copies, waits for them, and re-layouts: 68.5 us -> none  [pivot(): return jnp.sum(pivot_inverses * field[None], axis=1)]
    reduce_sum x14 -> x0, other arithmetic: 59.1 us -> none  [the longest x6 54.9 us: gather_beside(): return jnp.sum(couplings * beside[:, None], axis=(0, 2))]
    select_n x9 -> x0, other arithmetic: 54.7 us -> none  [the longest x4 52.3 us: shards(): sweep_field = jnp.where(chosen, current, sweep_field)]
    ppermute x24 -> x0, waiting for transfers between devices: 53.1 us -> none  [the longest x12 31.6 us: padded_2(): lax.ppermute(tail, axis, [(i, (i + 1) % count) for i in range(ends)])]
    all_gather x1 -> x0, blocking collectives: 37.2 us -> none  [shards(): values_all = lax.all_gather(own_values, ('gx', 'gy'), axis=0, tiled=True)]
  transfers between devices with their start and end apart: 25 -> 0, of which waited for: 11 -> 0; matrix products, arithmetic and copies ran while one was open for 14% -> 0% of each run, Pallas kernels for 0% -> 0%
where the time goes in v1:
time: 77.3 us; the launch traced here: 76.7 us
  Pallas kernels  68.8 us (89%)
  local copies, waits for them, and re-layouts  7.89 us (10%)
    pallas_call x1, Pallas kernels, shards(): pl.pallas_call(functools.partial(kernel, gx, gy), out_shape=jax.ShapeDtyp...  68.8 us
    unnamed x18, local copies, waits for them, and re-layouts  7.89 us

profile of v1, /device:TPU:0, one launch (start us, length us, event | category | flops | bytes accessed | tf_op | source)
XLA Modules:
  0.0 76.7 jit_solution(5167887995149450111)
XLA Ops:
  0.0 1.2 %copy.13.inverses = f32[64,16,16]{2,1,0:T(8,128)S(1)} copy(f32[64,16,16]{0,2,1:T(8,128)} %param.23) | data formatting | bytes 131072 | tf_op args[11]
  1.2 0.0 copy-start
  1.2 0.9 %copy-done = s32[32,8,256]{2,1,0:T(8,128)S(1)} copy-done((s32[32,8,256]{2,1,0:T(8,128)S(1)}, s32[32,8,256]{2,1,0:T(8,128)}, u32[]{:S(2)}) %copy-start) | copy-done | bytes 262168
  2.1 0.0 copy-start.1
  2.1 0.7 copy-done.1
  2.9 0.0 copy-start.2
  2.9 0.7 copy-done.2
  3.6 0.0 copy-start.3
  3.6 0.7 copy-done.3
  4.3 0.0 copy-start.4
  4.3 0.7 copy-done.4
  5.0 0.0 copy-start.5
  5.0 0.7 copy-done.5
  5.7 0.0 copy-start.6
  5.7 0.7 copy-done.6
  6.3 0.0 copy-start.7
  6.3 0.7 copy-done.7
  7.0 68.8 %precondition.1 = f32[3,32,8,256]{3,2,1,0:T(8,128)S(1)} custom-call(f32[3,32,8,256]{3,2,1,0:T(8,128)} %rhs.1, f32[6,3,3,32,8,256]{5,4,3,2,1,0:T(8,128)} %couplings.1, f32[3,3,32,8,256]{4,3,2,1,0:T(8,128)} %pivots.1, s32[32,8,256]{2,1,0:T(8,128)S(1)} %copy-done, s32[1,1024]{1,0:T(1,128)S(1)} %bitcast.7, s32[1,1024]{1,0:T(1,128)S(1)} %bitcast.8, ...), custom_call_target="tpu_custom_call" | custom-call | tf_op jit(solution)/shard_map/precondition/pallas_call | solution.py:471
  75.8 0.9 %copy.15 = f32[3,32,8,256]{3,2,1,0:T(8,128)} copy(f32[3,32,8,256]{3,2,1,0:T(8,128)S(1)} %precondition.1) | data formatting | bytes 1572864
Async XLA Ops:
  1.2 1.0 %copy-start = (s32[32,8,256]{2,1,0:T(8,128)S(1)}, s32[32,8,256]{2,1,0:T(8,128)}, u32[]{:S(2)}) copy-start(s32[32,8,256]{2,1,0:T(8,128)} %colours.1) | copy-start | bytes 786436
  2.1 0.7 copy-start.1
  2.9 0.7 copy-start.2
  3.6 0.7 copy-start.3
  4.3 0.7 copy-start.4
  5.0 0.7 copy-start.5
  5.7 0.7 copy-start.6
  6.3 0.7 copy-start.7

commit v2 on v1

--- a/solution.py
+++ b/solution.py
@@ -36,12 +36,6 @@
     return lax.dot_general(a, b, (((1,), (1,)), ((), ())), preferred_element_type=F32)
 
 
-def dot_exact(a, b):
-    return lax.dot_general(
-        a, b, (((1,), (0,)), ((), ())), precision=lax.Precision.HIGHEST, preferred_element_type=F32
-    )
-
-
 def one_hot(row, count):
     index = lax.broadcasted_iota(jnp.int32, (count, row.shape[1]), 0)
     return jnp.where(index == row, 1.0, 0.0).astype(BF16)
@@ -52,6 +46,19 @@
     gy,
     rhs,
     couplings,
+    pivots_in,
+    colours_in,
+    cells_in,
+    wells_in,
+    segs_in,
+    gather_in,
+    ret_in,
+    slots_in,
+    counts_in,
+    inverses_in,
+    out,
+    upper,
+    coup,
     pivots,
     colours,
     cells,
@@ -62,10 +69,7 @@
     slots,
     counts,
     inverses,
-    out,
-    coup,
     fld,
-    upper,
     acc,
     cx_edge,
     cy_edge,
@@ -79,12 +83,15 @@
     hot_r,
     hot_hi,
     hot_lo,
+    field_parts,
+    terms,
     totals,
     got_a,
     sum_a,
     got_b,
     values,
     load_sem,
+    small_sem,
     halo_send,
     halo_recv,
     a_send,
@@ -97,15 +104,36 @@
     d_recv,
 ):
     _, nz, cy, cx = rhs.shape
-    owned, seg, _ = inverses.shape
+    seg, _, owned = inverses.shape
+    perfs = cells.shape[1]
     ix = lax.axis_index("gx")
     iy = lax.axis_index("gy")
 
+    smalls = [
+        pltpu.make_async_copy(src, dst, small_sem.at[k])
+        for k, (src, dst) in enumerate(
+            (
+                (rhs, upper),
+                (pivots_in, pivots),
+                (colours_in, colours),
+                (cells_in, cells),
+                (wells_in, wells),
+                (segs_in, segs),
+                (gather_in, gather),
+                (ret_in, ret),
+                (slots_in, slots),
+                (counts_in, counts),
+                (inverses_in, inverses),
+            )
+        )
+    ]
     loads = [
         pltpu.make_async_copy(couplings.at[k], coup.at[k], load_sem.at[k]) for k in range(6)
     ]
-    for load in loads:
+    for load in smalls + loads:
         load.start()
+
+    barrier = pltpu.get_barrier_semaphore()
 
     @pl.when(ix == 0)
     def _():
@@ -123,7 +151,6 @@
     def _():
         yhalo[:, 1] = jnp.zeros_like(yhalo[:, 1])
 
-    barrier = pltpu.get_barrier_semaphore()
     for d in range(1, gx):
         pl.semaphore_signal(
             barrier, inc=1, device_id=(lax.rem(ix + d, gx), iy), device_id_type=MESH
@@ -200,77 +227,68 @@
                 x_add[side, i] = sum(cx_edge[side, i, j] * xhalo[slot, side, j] for j in range(3))
                 y_add[side, i] = sum(cy_edge[side, i, j] * yhalo[slot, side, j] for j in range(3))
 
-    def interior(base):
-        def step(z, carry):
-            total = [base[i, z] for i in range(3)]
-            for j in range(3):
-                here = fld[j, z + 1]
-                beside = (
-                    jnp.where(wide_lane == 0, 0.0, pltpu.roll(here, 1, 1)),
-                    jnp.where(wide_lane == cx - 1, 0.0, pltpu.roll(here, cx - 1, 1)),
-                    jnp.where(row == 0, 0.0, pltpu.roll(here, 1, 0)),
-                    jnp.where(row == cy - 1, 0.0, pltpu.roll(here, cy - 1, 0)),
-                    fld[j, z],
-                    fld[j, z + 2],
-                )
-                for i in range(3):
-                    for k in range(6):
-                        total[i] = total[i] - coup[k, i, j, z] * beside[k]
+    def interior(z, carry):
+        total = [upper[i, z] for i in range(3)]
+        for j in range(3):
+            here = fld[j, z + 1]
+            beside = (
+                jnp.where(wide_lane == 0, 0.0, pltpu.roll(here, 1, 1)),
+                jnp.where(wide_lane == cx - 1, 0.0, pltpu.roll(here, cx - 1, 1)),
+                jnp.where(row == 0, 0.0, pltpu.roll(here, 1, 0)),
+                jnp.where(row == cy - 1, 0.0, pltpu.roll(here, cy - 1, 0)),
+                fld[j, z],
+                fld[j, z + 2],
+            )
             for i in range(3):
-                acc[i, z] = total[i]
-            return carry
-
-        lax.fori_loop(0, nz, step, 0, unroll=2)
-
-    def finish(colour, slot, forward):
-        def step(z, packs):
-            current = []
-            for i in range(3):
-                first = jnp.where(lane == 0, pltpu.roll(x_add[0, i], LANES - z, 1), 0.0)
-                last = jnp.where(lane == LANES - 1, pltpu.roll(x_add[1, i], LANES - 1 - z, 1), 0.0)
-                pieces = [jnp.zeros((cy, LANES), F32)] * tiles
-                pieces[0] = pieces[0] + first
-                pieces[-1] = pieces[-1] + last
-                along_x = jnp.concatenate(pieces, axis=1) if tiles > 1 else pieces[0]
-                along_y = jnp.where(row == 0, y_add[0, i, pl.ds(z, 1), :], 0.0) + jnp.where(
-                    row == cy - 1, y_add[1, i, pl.ds(z, 1), :], 0.0
-                )
-                current.append(acc[i, z] - along_x - along_y)
-            chosen = colours[z] == colour
-            new = pivoted(z, current)
-            for i in range(3):
-                if forward:
-                    upper[i, z] = jnp.where(chosen, current[i], upper[i, z])
-                before = 0.0 if forward and colour == 3 else fld[i, z + 1]
-                new[i] = jnp.where(chosen, new[i], before)
-                fld[i, z + 1] = new[i]
-            if slot is None:
-                return packs
-            return emit(slot, z, new, packs)
-
-        packs = lax.fori_loop(0, nz, step, no_packs, unroll=2)
-        if slot is not None:
-            send_halo(slot, packs)
+                for k in range(6):
+                    total[i] = total[i] - coup[k, i, j, z] * beside[k]
+        for i in range(3):
+            acc[i, z] = total[i]
+        return carry
+
+    def finish(turn, colour, z, packs):
+        current = []
+        for i in range(3):
+            first = jnp.where(lane == 0, pltpu.roll(x_add[0, i], LANES - z, 1), 0.0)
+            last = jnp.where(lane == LANES - 1, pltpu.roll(x_add[1, i], LANES - 1 - z, 1), 0.0)
+            pieces = [jnp.zeros((cy, LANES), F32)] * tiles
+            pieces[0] = pieces[0] + first
+            pieces[-1] = pieces[-1] + last
+            along_x = jnp.concatenate(pieces, axis=1) if tiles > 1 else pieces[0]
+            along_y = jnp.where(row == 0, y_add[0, i, pl.ds(z, 1), :], 0.0) + jnp.where(
+                row == cy - 1, y_add[1, i, pl.ds(z, 1), :], 0.0
+            )
+            current.append(acc[i, z] - along_x - along_y)
+        chosen = colours[z] == colour
+        new = pivoted(z, current)
+        kept = jnp.where(turn == 3, 0.0, 1.0)
+        for i in range(3):
+            upper[i, z] = jnp.where(chosen, current[i], upper[i, z])
+            new[i] = jnp.where(chosen, new[i], fld[i, z + 1] * kept)
+            fld[i, z + 1] = new[i]
+        return emit(turn, z, new, packs)
 
     def first(z, packs):
         chosen = colours[z] == 0
-        field = [rhs[i, z] for i in range(3)]
-        new = pivoted(z, field)
+        new = pivoted(z, [upper[i, z] for i in range(3)])
         for i in range(3):
-            upper[i, z] = field[i]
             new[i] = jnp.where(chosen, new[i], 0.0)
             fld[i, z + 1] = new[i]
         return emit(0, z, new, packs)
 
-    packs = lax.fori_loop(0, nz, first, no_packs, unroll=2)
+    for load in smalls[:3]:
+        load.wait()
+    packs = lax.fori_loop(0, nz, first, no_packs, unroll=8)
     pl.semaphore_wait(barrier, gx + gy - 2)
     send_halo(0, packs)
 
+    for load in smalls[3:]:
+        load.wait()
     cell = cells[...]
+    key = wells[...] * seg + segs[...]
     hot_x[...] = one_hot(cell & (cx - 1), cx)
     hot_r[...] = one_hot(cell >> shift_of(cx), nz * cy)
     per_owner = owned * seg // LANES
-    key = wells[...] * seg + segs[...]
     high = key >> shift_of(LANES)
     owner = high >> shift_of(per_owner)
     placed = (owner & (gy - 1)) * gx + (owner >> shift_of(gy))
@@ -281,7 +299,7 @@
     for load in loads:
         load.wait()
 
-    for i in range(3):
+    def pack_edges(i, carry):
         for j in range(3):
 
             def pack(z, carry):
@@ -294,30 +312,48 @@
                 cy_edge[1, i, j, pl.ds(z, 1), :] = coup[3, i, j, z, cy - 1 : cy, :]
                 return left, right
 
-            left, right = lax.fori_loop(0, nz, pack, no_packs[:2], unroll=4)
+            left, right = lax.fori_loop(0, nz, pack, no_packs[:2], unroll=16)
             cx_edge[0, i, j] = left
             cx_edge[1, i, j] = right
-
-    slot = 0
-    for colour in (1, 2, 3):
-        interior(rhs)
-        take_halo(slot)
-        slot += 1
-        finish(colour, slot, True)
-    for colour in (2, 1, 0):
-        interior(upper)
-        take_halo(slot)
-        slot += 1
-        finish(colour, slot if colour > 0 else None, False)
-
-    term = jnp.zeros(hot_r.shape, F32)
+        return carry
+
+    lax.fori_loop(0, 3, pack_edges, 0)
+
+    def one_turn(turn, carry):
+        colour = 3 - jnp.abs(turn - 3)
+        lax.fori_loop(0, nz, interior, 0, unroll=4)
+        take_halo(turn - 1)
+        packs = lax.fori_loop(
+            0, nz, functools.partial(finish, turn, colour), no_packs, unroll=8
+        )
+
+        @pl.when(turn < 6)
+        def _():
+            send_halo(turn, packs)
+
+        return carry
+
+    lax.fori_loop(1, 7, one_turn, 0)
+
     for u in range(3):
-        field = fld[u, 1 : nz + 1].reshape(nz * cy, cx)
-        read = sum(dot_nn(part, hot_x[...]) for part in parts_of(field))
-        term = term + read * gather[u : u + 1, :]
-    term = jnp.sum(term * hot_r[...].astype(F32), axis=0, keepdims=True)
-    spread = hot_lo[...].astype(F32) * term
-    sums = sum(dot_nt(hot_hi[...], part) for part in parts_of(spread))
+        for k, part in enumerate(parts_of(fld[u, 1 : nz + 1].reshape(nz * cy, cx), 2)):
+            field_parts[u, k] = part
+    chunk = min(perfs, 256)
+    row_index = lax.broadcasted_iota(jnp.int32, (nz * cy, chunk), 0)
+
+    def read_terms(c, carry):
+        at = pl.ds(pl.multiple_of(c * chunk, chunk), chunk)
+        column = hot_x[:, at]
+        term = jnp.zeros((nz * cy, chunk), F32)
+        for u in range(3):
+            read = dot_nn(field_parts[u, 0], column) + dot_nn(field_parts[u, 1], column)
+            term = term + read * gather[u : u + 1, at]
+        there = cells[:, at] >> shift_of(cx)
+        terms[:, at] = jnp.sum(jnp.where(row_index == there, term, 0.0), axis=0, keepdims=True)
+        return carry
+
+    lax.fori_loop(0, perfs // chunk, read_terms, 0)
+    sums = sum(dot_nt(hot_hi[...], hot_lo[...] * part) for part in parts_of(terms[...]))
     totals[...] = sums.reshape(totals.shape)
 
     def along_gy(src, dst, send, recv, d):
@@ -357,21 +393,22 @@
 
     slot_row = own_row(slots) - first_well
     count_row = own_row(counts)
-    by_slot = lax.broadcasted_iota(jnp.int32, (owned, owned), 0)
-    by_well = lax.broadcasted_iota(jnp.int32, (owned, owned), 1)
-    order = jnp.where(slot_row == by_slot, 1.0, 0.0)
-    live = jnp.sum(jnp.where(slot_row == by_slot, count_row, 0), axis=1, keepdims=True)
-    slot_column = jnp.sum(jnp.where(by_slot == by_well, slot_row, 0), axis=1, keepdims=True)
-    back_index = lax.broadcasted_iota(jnp.int32, (owned, owned * seg), 1) >> shift_of(seg)
-    back = jnp.where(back_index == slot_column, 1.0, 0.0)
+    down = lax.broadcasted_iota(jnp.int32, (owned, owned), 0)
+    across = lax.broadcasted_iota(jnp.int32, (owned, owned), 1)
+    slot_column = jnp.sum(jnp.where(down == across, slot_row, 0), axis=1, keepdims=True)
+    count_column = jnp.sum(jnp.where(down == across, count_row, 0), axis=1, keepdims=True)
+    to_slot = jnp.where(slot_row == down, 1.0, 0.0).astype(BF16)
+    of_well = slot_column == across
+    to_well = jnp.where(of_well, 1.0, 0.0).astype(BF16)
+    live = jnp.sum(jnp.where(of_well, count_column, 0), axis=0, keepdims=True)
+    alive = lax.broadcasted_iota(jnp.int32, (seg, owned), 0) < live
     wells_row = LANES // seg
     lane_of = lax.broadcasted_iota(jnp.int32, (owned, LANES), 1)
     well_of = lax.broadcasted_iota(jnp.int32, (owned, LANES), 0)
     mine = (lane_of >> shift_of(seg)) == (well_of & (wells_row - 1))
-    fold_from = lax.broadcasted_iota(jnp.int32, (LANES, seg), 0)
-    fold_to = lax.broadcasted_iota(jnp.int32, (LANES, seg), 1)
-    fold = jnp.where((fold_from & (seg - 1)) == fold_to, 1.0, 0.0)
-    segment = lax.broadcasted_iota(jnp.int32, (owned, seg), 1)
+    fold_from = lax.broadcasted_iota(jnp.int32, (seg, LANES), 1)
+    fold_to = lax.broadcasted_iota(jnp.int32, (seg, LANES), 0)
+    fold = jnp.where((fold_from & (seg - 1)) == fold_to, 1.0, 0.0).astype(BF16)
 
     for copy in copies_a:
         copy.wait_recv()
@@ -392,15 +429,15 @@
         own = own + got_b[d]
 
     rows = jnp.broadcast_to(own[:, None, :], (per_owner, wells_row, LANES)).reshape(owned, LANES)
-    by_segment = dot_exact(dot_exact(order, jnp.where(mine, rows, 0.0)), fold)
-    by_segment = jnp.where(segment < live, by_segment, 0.0)
-    solved = jnp.sum(inverses[...] * by_segment[:, None, :], axis=2, keepdims=True)
-    inner = lax.broadcasted_iota(jnp.int32, (owned, seg, LANES), 1)
-    outer = lax.broadcasted_iota(jnp.int32, (owned, seg, LANES), 2) & (seg - 1)
-    alive = (inner == outer) & (inner < live[:, :, None])
-    solved = jnp.where(alive, solved, 0.0).reshape(owned * seg, LANES)
-    spread_back = jnp.where(mine, dot_exact(back, solved), 0.0)
-    values[iy, ix] = jnp.sum(spread_back.reshape(per_owner, wells_row, LANES), axis=1)
+    by_well = sum(dot_nt(fold, part) for part in parts_of(jnp.where(mine, rows, 0.0)))
+    by_slot = sum(dot_nt(part, to_slot) for part in parts_of(by_well))
+    by_slot = jnp.where(alive, by_slot, 0.0)
+    solved = jnp.sum(inverses[...] * by_slot[None], axis=1)
+    solved = jnp.where(alive, solved, 0.0)
+    solved = sum(dot_nt(to_well, part) for part in parts_of(solved))
+    solved = sum(dot_nn(part, fold) for part in parts_of(solved))
+    solved = jnp.where(mine, solved, 0.0)
+    values[iy, ix] = jnp.sum(solved.reshape(per_owner, wells_row, LANES), axis=1)
 
     def sent_c(d):
         return along_gx(values.at[iy, ix], values.at[iy, ix], c_send, c_recv, d)
@@ -427,14 +464,19 @@
         due_d(d).wait_recv()
 
     table = values[...].reshape(gx * gy * per_owner, LANES)
-    read = sum(dot_nn(part, hot_lo[...]) for part in parts_of(table))
-    at_perfs = jnp.sum(read * hot_hi[...].astype(F32), axis=0, keepdims=True)
+    table_parts = parts_of(table)
+    for c in range(perfs // chunk):
+        at = pl.ds(c * chunk, chunk)
+        column = hot_lo[:, at]
+        read = sum(dot_nn(part, column) for part in table_parts)
+        terms[:, at] = jnp.sum(read * hot_hi[:, at].astype(F32), axis=0, keepdims=True)
+    at_perfs = terms[...]
     for u in range(3):
-        weights = hot_x[...].astype(F32) * (ret[u : u + 1, :] * at_perfs)
-        change = sum(dot_nt(hot_r[...], part) for part in parts_of(weights))
+        weights = parts_of(ret[u : u + 1, :] * at_perfs, 2)
+        change = sum(dot_nt(hot_r[...], hot_x[...] * part) for part in weights)
         out[u] = fld[u, 1 : nz + 1] - change.reshape(nz, cy, cx)
 
-    for done in range(slot):
+    for done in range(6):
         for copy, inside in halo_copies(done):
             pl.when(inside)(copy.wait_send)
     for copy in copies_a + copies_b:
@@ -466,36 +508,52 @@
     perfs = perf_cells.shape[0]
     per_owner = owned * seg // LANES
     high = gx * gy * per_owner
-    vmem = pl.BlockSpec(memory_space=pltpu.VMEM)
+    hbm = pl.BlockSpec(memory_space=pltpu.HBM)
     dma = pltpu.SemaphoreType.DMA
+    operands = (
+        rhs_field,
+        couplings,
+        pivot_inverses,
+        colours,
+        perf_cells.reshape(1, perfs),
+        perf_wells.reshape(1, perfs),
+        perf_segments.reshape(1, perfs),
+        perf_gather,
+        perf_return,
+        well_slot.reshape(-1, LANES),
+        seg_count.reshape(-1, LANES),
+        jnp.transpose(well_inverses, (1, 2, 0)),
+    )
     return pl.pallas_call(
         functools.partial(kernel, gx, gy),
         out_shape=jax.ShapeDtypeStruct(rhs_field.shape, F32),
-        in_specs=[vmem, pl.BlockSpec(memory_space=pl.ANY)] + [vmem] * 10,
-        out_specs=vmem,
-        scratch_shapes=[
-            pltpu.VMEM(couplings.shape, F32),
+        in_specs=[hbm] * len(operands),
+        out_specs=pl.BlockSpec(memory_space=pltpu.VMEM),
+        scratch_shapes=[pltpu.VMEM(x.shape, x.dtype) for x in operands]
+        + [
             pltpu.VMEM((3, nz + 2, cy, cx), F32),
-            pltpu.VMEM((3, nz, cy, cx), F32),
             pltpu.VMEM((3, nz, cy, cx), F32),
             pltpu.VMEM((2, 3, 3, cy, LANES), F32),
             pltpu.VMEM((2, 3, 3, nz, cx), F32),
             pltpu.VMEM((2, 3, cy, LANES), F32),
             pltpu.VMEM((2, 3, nz, cx), F32),
             pltpu.VMEM((6, 2, 3, cy, LANES), F32),
-            pltpu.VMEM((6, 2, 3, nz, cx), F32),
+            pltpu.VMEM((7, 2, 3, nz, cx), F32),
             pltpu.VMEM((6, 2, 3, cy, LANES), F32),
             pltpu.VMEM((6, 2, 3, nz, cx), F32),
             pltpu.VMEM((cx, perfs), BF16),
             pltpu.VMEM((nz * cy, perfs), BF16),
             pltpu.VMEM((high, perfs), BF16),
             pltpu.VMEM((LANES, perfs), BF16),
+            pltpu.VMEM((3, 2, nz * cy, cx), BF16),
+            pltpu.VMEM((1, perfs), F32),
             pltpu.VMEM((gy, gx, per_owner, LANES), F32),
             pltpu.VMEM((gy, gx, per_owner, LANES), F32),
             pltpu.VMEM((gx, per_owner, LANES), F32),
             pltpu.VMEM((gx, per_owner, LANES), F32),
             pltpu.VMEM((gy, gx, per_owner, LANES), F32),
             dma((6,)),
+            dma((11,)),
             dma((6, 4)),
             dma((6, 4)),
             dma((gy,)),
@@ -508,23 +566,10 @@
             dma((gy,)),
         ],
         compiler_params=pltpu.CompilerParams(
-            collective_id=0, has_side_effects=True, vmem_limit_bytes=52 * 2**20
+            collective_id=0, has_side_effects=True, vmem_limit_bytes=63 * 2**20 + 2**19
         ),
         name="precondition",
-    )(
-        rhs_field,
-        couplings,
-        pivot_inverses,
-        colours,
-        perf_cells.reshape(1, perfs),
-        perf_wells.reshape(1, perfs),
-        perf_segments.reshape(1, perfs),
-        perf_gather,
-        perf_return,
-        well_slot.reshape(-1, LANES),
-        seg_count.reshape(-1, LANES),
-        well_inverses,
-    )
+    )(*operands)
 
 
 def solution(mesh):

time: 77.3 us -> 58.2 us (0.75)
  Pallas kernels: 68.8 us -> 56 us
  local copies, waits for them, and re-layouts: 7.89 us -> 2.06 us
    pallas_call x1, Pallas kernels: 68.8 us -> 56 us  [shards(): pl.pallas_call(functools.partial(kernel, gx, gy), out_shape=jax.ShapeDtyp...]
    unnamed x18 -> x1, local copies, waits for them, and re-layouts: 7.89 us -> 2.06 us
where the time goes in v2:
time: 58.2 us; the launch traced here: 58.1 us
  Pallas kernels  56 us (96%)
  local copies, waits for them, and re-layouts  2.06 us (4%)
    pallas_call x1, Pallas kernels, shards(): pl.pallas_call(functools.partial(kernel, gx, gy), out_shape=jax.ShapeDtyp...  56 us
    unnamed x1, local copies, waits for them, and re-layouts  2.06 us

profile of v2, /device:TPU:0, one launch (start us, length us, event | category | flops | bytes accessed | tf_op | source)
XLA Modules:
  0.0 58.1 jit_solution(36649713539301176)
XLA Ops:
  0.0 56.0 %precondition.1 = f32[3,32,8,256]{3,2,1,0:T(8,128)} custom-call(f32[3,32,8,256]{3,2,1,0:T(8,128)} %rhs.1, f32[6,3,3,32,8,256]{5,4,3,2,1,0:T(8,128)} %couplings.1, f32[3,3,32,8,256]{4,3,2,1,0:T(8,128)} %pivots_in.1, s32[32,8,256]{2,1,0:T(8,128)} %colours_in.1, s32[1,1024]{1,0:T(1,128)} %bitcast.9, s32[1,1024]{1,0:T(1,128)} %bitcast.10, s32[1,1024]{1,0:T(1,128)} %bitcast.11, ...), custom_call_target="tpu_custom_call" | custom-call | tf_op jit(solution)/shard_map/precondition/pallas_call | solution.py:527
  56.0 2.1 %copy.14 = f32[3,32,8,256]{3,2,1,0:T(8,128)} copy(f32[3,32,8,256]{3,2,1,0:T(8,128)} %precondition.1) | data formatting | bytes 1572864

commit v3 on v2

--- a/solution.py
+++ b/solution.py
@@ -92,8 +92,10 @@
     values,
     load_sem,
     small_sem,
-    halo_send,
-    halo_recv,
+    x_send,
+    x_recv,
+    y_send,
+    y_recv,
     a_send,
     a_recv,
     b_send,
@@ -106,6 +108,7 @@
     _, nz, cy, cx = rhs.shape
     seg, _, owned = inverses.shape
     perfs = cells.shape[1]
+    depth = 8
     ix = lax.axis_index("gx")
     iy = lax.axis_index("gy")
 
@@ -190,38 +193,61 @@
 
     no_packs = tuple(jnp.zeros((cy, LANES), F32) for _ in range(6))
 
-    def halo_copies(slot):
+    def x_copies(slot):
         found = []
-        for side, (buffers, there, inside) in enumerate(
-            (
-                ((xsend, xhalo), (ix + 1, iy), ix < gx - 1),
-                ((xsend, xhalo), (ix - 1, iy), ix > 0),
-                ((ysend, yhalo), (ix, iy + 1), iy < gy - 1),
-                ((ysend, yhalo), (ix, iy - 1), iy > 0),
-            )
-        ):
+        for side, there, inside in ((0, ix + 1, ix < gx - 1), (1, ix - 1, ix > 0)):
             copy = pltpu.make_async_remote_copy(
-                src_ref=buffers[0].at[slot, side % 2],
-                dst_ref=buffers[1].at[slot, side % 2],
-                send_sem=halo_send.at[slot, side],
-                recv_sem=halo_recv.at[slot, side],
-                device_id=there,
+                src_ref=xsend.at[slot, side],
+                dst_ref=xhalo.at[slot, side],
+                send_sem=x_send.at[slot, side],
+                recv_sem=x_recv.at[slot, side],
+                device_id=(there, iy),
                 device_id_type=MESH,
             )
             found.append((copy, inside))
         return found
 
+    def y_copies(slot, c):
+        found = []
+        layers = pl.ds(pl.multiple_of(c * depth, depth), depth)
+        for side, there, inside in ((0, iy + 1, iy < gy - 1), (1, iy - 1, iy > 0)):
+            copy = pltpu.make_async_remote_copy(
+                src_ref=ysend.at[slot, side, :, layers, :],
+                dst_ref=yhalo.at[slot, side, :, layers, :],
+                send_sem=y_send.at[slot, c, side],
+                recv_sem=y_recv.at[slot, c, side],
+                device_id=(ix, there),
+                device_id_type=MESH,
+            )
+            found.append((copy, inside))
+        return found
+
+    def sweep_layers(slot, body):
+        def some(c, packs):
+            for k in range(depth):
+                packs = body(c * depth + k, packs)
+
+            @pl.when(slot < 6)
+            def _():
+                for copy, inside in y_copies(slot, c):
+                    pl.when(inside)(copy.start)
+
+            return packs
+
+        return lax.fori_loop(0, nz // depth, some, no_packs)
+
     def send_halo(slot, packs):
         for j in range(3):
             xsend[slot, 0, j] = packs[j]
             xsend[slot, 1, j] = packs[3 + j]
-        for copy, inside in halo_copies(slot):
+        for copy, inside in x_copies(slot):
             pl.when(inside)(copy.start)
 
     def take_halo(slot):
-        copies = halo_copies(slot)
-        for side in range(4):
-            pl.when(copies[side ^ 1][1])(copies[side][0].wait_recv)
+        copies = [x_copies(slot)] + [y_copies(slot, c) for c in range(nz // depth)]
+        for pair in copies:
+            pl.when(pair[1][1])(pair[0][0].wait_recv)
+            pl.when(pair[0][1])(pair[1][0].wait_recv)
         for side in range(2):
             for i in range(3):
                 x_add[side, i] = sum(cx_edge[side, i, j] * xhalo[slot, side, j] for j in range(3))
@@ -278,8 +304,8 @@
 
     for load in smalls[:3]:
         load.wait()
-    packs = lax.fori_loop(0, nz, first, no_packs, unroll=8)
     pl.semaphore_wait(barrier, gx + gy - 2)
+    packs = sweep_layers(0, first)
     send_halo(0, packs)
 
     for load in smalls[3:]:
@@ -296,7 +322,7 @@
     hot_hi[...] = one_hot(high, gx * gy * per_owner)
     hot_lo[...] = one_hot(key & (LANES - 1), LANES)
 
-    for load in loads:
+    for load in loads[:4]:
         load.wait()
 
     def pack_edges(i, carry):
@@ -318,14 +344,14 @@
         return carry
 
     lax.fori_loop(0, 3, pack_edges, 0)
+    for load in loads[4:]:
+        load.wait()
 
     def one_turn(turn, carry):
         colour = 3 - jnp.abs(turn - 3)
         lax.fori_loop(0, nz, interior, 0, unroll=4)
         take_halo(turn - 1)
-        packs = lax.fori_loop(
-            0, nz, functools.partial(finish, turn, colour), no_packs, unroll=8
-        )
+        packs = sweep_layers(turn, functools.partial(finish, turn, colour))
 
         @pl.when(turn < 6)
         def _():
@@ -477,8 +503,9 @@
         out[u] = fld[u, 1 : nz + 1] - change.reshape(nz, cy, cx)
 
     for done in range(6):
-        for copy, inside in halo_copies(done):
-            pl.when(inside)(copy.wait_send)
+        for pair in [x_copies(done)] + [y_copies(done, c) for c in range(nz // depth)]:
+            for copy, inside in pair:
+                pl.when(inside)(copy.wait_send)
     for copy in copies_a + copies_b:
         copy.wait_send()
     for d in range(1, gx):
@@ -554,8 +581,10 @@
             pltpu.VMEM((gy, gx, per_owner, LANES), F32),
             dma((6,)),
             dma((11,)),
-            dma((6, 4)),
-            dma((6, 4)),
+            dma((6, 2)),
+            dma((6, 2)),
+            dma((6, nz // 8, 2)),
+            dma((6, nz // 8, 2)),
             dma((gy,)),
             dma((gy,)),
             dma((gx,)),

time: 58.2 us -> 58 us (level)
  no operation moved by 1% of the time
where the time goes in v3:
time: 58 us; the launch traced here: 57.9 us
  Pallas kernels  55.8 us (96%)
  local copies, waits for them, and re-layouts  2.06 us (4%)
    pallas_call x1, Pallas kernels, shards(): pl.pallas_call(functools.partial(kernel, gx, gy), out_shape=jax.ShapeDtyp...  55.8 us
    unnamed x1, local copies, waits for them, and re-layouts  2.06 us

profile of v3, /device:TPU:0, one launch (start us, length us, event | category | flops | bytes accessed | tf_op | source)
XLA Modules:
  0.0 57.9 jit_solution(7113087253956153579)
XLA Ops:
  0.0 55.8 %precondition.1 = f32[3,32,8,256]{3,2,1,0:T(8,128)} custom-call(f32[3,32,8,256]{3,2,1,0:T(8,128)} %rhs.1, f32[6,3,3,32,8,256]{5,4,3,2,1,0:T(8,128)} %couplings.1, f32[3,3,32,8,256]{4,3,2,1,0:T(8,128)} %pivots_in.1, s32[32,8,256]{2,1,0:T(8,128)} %colours_in.1, s32[1,1024]{1,0:T(1,128)} %bitcast.9, s32[1,1024]{1,0:T(1,128)} %bitcast.10, s32[1,1024]{1,0:T(1,128)} %bitcast.11, ...), custom_call_target="tpu_custom_call" | custom-call | tf_op jit(solution)/shard_map/precondition/pallas_call | solution.py:554
  55.8 2.1 %copy.14 = f32[3,32,8,256]{3,2,1,0:T(8,128)} copy(f32[3,32,8,256]{3,2,1,0:T(8,128)} %precondition.1) | data formatting | bytes 1572864

commit v4 on v3

--- a/solution.py
+++ b/solution.py
@@ -86,9 +86,7 @@
     field_parts,
     terms,
     totals,
-    got_a,
-    sum_a,
-    got_b,
+    got,
     values,
     load_sem,
     small_sem,
@@ -100,10 +98,6 @@
     a_recv,
     b_send,
     b_recv,
-    c_send,
-    c_recv,
-    d_send,
-    d_recv,
 ):
     _, nz, cy, cx = rhs.shape
     seg, _, owned = inverses.shape
@@ -111,6 +105,12 @@
     depth = 8
     ix = lax.axis_index("gx")
     iy = lax.axis_index("gy")
+    count = gx * gy
+    me = ix * gy + iy
+
+    def peer(d):
+        there = lax.rem(me + d, count)
+        return lax.div(there, gy), lax.rem(there, gy)
 
     smalls = [
         pltpu.make_async_copy(src, dst, small_sem.at[k])
@@ -154,14 +154,11 @@
     def _():
         yhalo[:, 1] = jnp.zeros_like(yhalo[:, 1])
 
-    for d in range(1, gx):
-        pl.semaphore_signal(
-            barrier, inc=1, device_id=(lax.rem(ix + d, gx), iy), device_id_type=MESH
-        )
-    for d in range(1, gy):
-        pl.semaphore_signal(
-            barrier, inc=1, device_id=(ix, lax.rem(iy + d, gy)), device_id_type=MESH
-        )
+    def greet(d, carry):
+        pl.semaphore_signal(barrier, inc=1, device_id=peer(d), device_id_type=MESH)
+        return carry
+
+    lax.fori_loop(1, count, greet, 0)
 
     lane = lax.broadcasted_iota(jnp.int32, (cy, LANES), 1)
     wide_lane = lax.broadcasted_iota(jnp.int32, (cy, cx), 1)
@@ -207,15 +204,14 @@
             found.append((copy, inside))
         return found
 
-    def y_copies(slot, c):
+    def y_copies(slot, layers):
         found = []
-        layers = pl.ds(pl.multiple_of(c * depth, depth), depth)
         for side, there, inside in ((0, iy + 1, iy < gy - 1), (1, iy - 1, iy > 0)):
             copy = pltpu.make_async_remote_copy(
                 src_ref=ysend.at[slot, side, :, layers, :],
                 dst_ref=yhalo.at[slot, side, :, layers, :],
-                send_sem=y_send.at[slot, c, side],
-                recv_sem=y_recv.at[slot, c, side],
+                send_sem=y_send.at[slot, side],
+                recv_sem=y_recv.at[slot, side],
                 device_id=(ix, there),
                 device_id_type=MESH,
             )
@@ -229,7 +225,8 @@
 
             @pl.when(slot < 6)
             def _():
-                for copy, inside in y_copies(slot, c):
+                layers = pl.ds(pl.multiple_of(c * depth, depth), depth)
+                for copy, inside in y_copies(slot, layers):
                     pl.when(inside)(copy.start)
 
             return packs
@@ -244,8 +241,7 @@
             pl.when(inside)(copy.start)
 
     def take_halo(slot):
-        copies = [x_copies(slot)] + [y_copies(slot, c) for c in range(nz // depth)]
-        for pair in copies:
+        for pair in (x_copies(slot), y_copies(slot, slice(None))):
             pl.when(pair[1][1])(pair[0][0].wait_recv)
             pl.when(pair[0][1])(pair[1][0].wait_recv)
         for side in range(2):
@@ -304,7 +300,7 @@
 
     for load in smalls[:3]:
         load.wait()
-    pl.semaphore_wait(barrier, gx + gy - 2)
+    pl.semaphore_wait(barrier, count - 1)
     packs = sweep_layers(0, first)
     send_halo(0, packs)
 
@@ -317,9 +313,9 @@
     per_owner = owned * seg // LANES
     high = key >> shift_of(LANES)
     owner = high >> shift_of(per_owner)
-    placed = (owner & (gy - 1)) * gx + (owner >> shift_of(gy))
-    high = placed * per_owner + (high & (per_owner - 1))
-    hot_hi[...] = one_hot(high, gx * gy * per_owner)
+    offset = (owner - me) & (count - 1)
+    high = offset * per_owner + (high & (per_owner - 1))
+    hot_hi[...] = one_hot(high, count * per_owner)
     hot_lo[...] = one_hot(key & (LANES - 1), LANES)
 
     for load in loads[:4]:
@@ -382,34 +378,23 @@
     sums = sum(dot_nt(hot_hi[...], hot_lo[...] * part) for part in parts_of(terms[...]))
     totals[...] = sums.reshape(totals.shape)
 
-    def along_gy(src, dst, send, recv, d):
+    def sent_totals(d, blocks=1):
         return pltpu.make_async_remote_copy(
-            src_ref=src,
-            dst_ref=dst,
-            send_sem=send.at[d],
-            recv_sem=recv.at[d],
-            device_id=(ix, lax.rem(iy + d, gy)),
+            src_ref=totals.at[pl.ds(d, blocks)],
+            dst_ref=got.at[pl.ds(d, blocks)],
+            send_sem=a_send,
+            recv_sem=a_recv,
+            device_id=peer(d),
             device_id_type=MESH,
         )
 
-    def along_gx(src, dst, send, recv, d):
-        return pltpu.make_async_remote_copy(
-            src_ref=src,
-            dst_ref=dst,
-            send_sem=send.at[d],
-            recv_sem=recv.at[d],
-            device_id=(lax.rem(ix + d, gx), iy),
-            device_id_type=MESH,
-        )
-
-    copies_a = [
-        along_gy(totals.at[lax.rem(iy + d, gy)], got_a.at[d], a_send, a_recv, d)
-        for d in range(1, gy)
-    ]
-    for copy in copies_a:
-        copy.start()
-
-    first_well = (ix * gy + iy) * owned
+    def start_totals(d, carry):
+        sent_totals(d).start()
+        return carry
+
+    lax.fori_loop(1, count, start_totals, 0)
+
+    first_well = me * owned
     at_row = lax.div(first_well, LANES)
     at_lane = lax.rem(first_well, LANES)
 
@@ -436,23 +421,8 @@
     fold_to = lax.broadcasted_iota(jnp.int32, (seg, LANES), 0)
     fold = jnp.where((fold_from & (seg - 1)) == fold_to, 1.0, 0.0).astype(BF16)
 
-    for copy in copies_a:
-        copy.wait_recv()
-    summed = totals[iy]
-    for d in range(1, gy):
-        summed = summed + got_a[d]
-    sum_a[...] = summed
-    copies_b = [
-        along_gx(sum_a.at[lax.rem(ix + d, gx)], got_b.at[d], b_send, b_recv, d)
-        for d in range(1, gx)
-    ]
-    for copy in copies_b:
-        copy.start()
-    for copy in copies_b:
-        copy.wait_recv()
-    own = sum_a[ix]
-    for d in range(1, gx):
-        own = own + got_b[d]
+    sent_totals(1, count - 1).wait_recv()
+    own = totals[0] + jnp.sum(got[1:], axis=0)
 
     rows = jnp.broadcast_to(own[:, None, :], (per_owner, wells_row, LANES)).reshape(owned, LANES)
     by_well = sum(dot_nt(fold, part) for part in parts_of(jnp.where(mine, rows, 0.0)))
@@ -463,33 +433,35 @@
     solved = sum(dot_nt(to_well, part) for part in parts_of(solved))
     solved = sum(dot_nn(part, fold) for part in parts_of(solved))
     solved = jnp.where(mine, solved, 0.0)
-    values[iy, ix] = jnp.sum(solved.reshape(per_owner, wells_row, LANES), axis=1)
-
-    def sent_c(d):
-        return along_gx(values.at[iy, ix], values.at[iy, ix], c_send, c_recv, d)
-
-    def due_c(d):
-        there = lax.rem(ix + gx - d, gx)
-        return along_gx(values.at[iy, there], values.at[iy, there], c_send, c_recv, d)
-
-    for d in range(1, gx):
-        sent_c(d).start()
-    for d in range(1, gx):
-        due_c(d).wait_recv()
-
-    def sent_d(d):
-        return along_gy(values.at[iy], values.at[iy], d_send, d_recv, d)
-
-    def due_d(d):
-        there = lax.rem(iy + gy - d, gy)
-        return along_gy(values.at[there], values.at[there], d_send, d_recv, d)
-
-    for d in range(1, gy):
-        sent_d(d).start()
-    for d in range(1, gy):
-        due_d(d).wait_recv()
-
-    table = values[...].reshape(gx * gy * per_owner, LANES)
+    values[0] = jnp.sum(solved.reshape(per_owner, wells_row, LANES), axis=1)
+
+    def sent_values(d):
+        return pltpu.make_async_remote_copy(
+            src_ref=values.at[pl.ds(0, 1)],
+            dst_ref=values.at[pl.ds(count - d, 1)],
+            send_sem=b_send,
+            recv_sem=b_recv,
+            device_id=peer(d),
+            device_id_type=MESH,
+        )
+
+    def start_values(d, carry):
+        sent_values(d).start()
+        return carry
+
+    lax.fori_loop(1, count, start_values, 0)
+    others = values.at[pl.ds(1, count - 1)]
+    all_values = pltpu.make_async_remote_copy(
+        src_ref=others,
+        dst_ref=others,
+        send_sem=b_send,
+        recv_sem=b_recv,
+        device_id=peer(1),
+        device_id_type=MESH,
+    )
+    all_values.wait_recv()
+
+    table = values[...].reshape(count * per_owner, LANES)
     table_parts = parts_of(table)
     for c in range(perfs // chunk):
         at = pl.ds(c * chunk, chunk)
@@ -503,15 +475,11 @@
         out[u] = fld[u, 1 : nz + 1] - change.reshape(nz, cy, cx)
 
     for done in range(6):
-        for pair in [x_copies(done)] + [y_copies(done, c) for c in range(nz // depth)]:
+        for pair in (x_copies(done), y_copies(done, slice(None))):
             for copy, inside in pair:
                 pl.when(inside)(copy.wait_send)
-    for copy in copies_a + copies_b:
-        copy.wait_send()
-    for d in range(1, gx):
-        sent_c(d).wait_send()
-    for d in range(1, gy):
-        sent_d(d).wait_send()
+    sent_totals(1, count - 1).wait_send()
+    all_values.wait_send()
 
 
 def shards(
@@ -574,25 +542,19 @@
             pltpu.VMEM((LANES, perfs), BF16),
             pltpu.VMEM((3, 2, nz * cy, cx), BF16),
             pltpu.VMEM((1, perfs), F32),
-            pltpu.VMEM((gy, gx, per_owner, LANES), F32),
-            pltpu.VMEM((gy, gx, per_owner, LANES), F32),
-            pltpu.VMEM((gx, per_owner, LANES), F32),
-            pltpu.VMEM((gx, per_owner, LANES), F32),
-            pltpu.VMEM((gy, gx, per_owner, LANES), F32),
+            pltpu.VMEM((gx * gy, per_owner, LANES), F32),
+            pltpu.VMEM((gx * gy, per_owner, LANES), F32),
+            pltpu.VMEM((gx * gy, per_owner, LANES), F32),
             dma((6,)),
             dma((11,)),
             dma((6, 2)),
             dma((6, 2)),
-            dma((6, nz // 8, 2)),
-            dma((6, nz // 8, 2)),
-            dma((gy,)),
-            dma((gy,)),
-            dma((gx,)),
-            dma((gx,)),
-            dma((gx,)),
-            dma((gx,)),
-            dma((gy,)),
-            dma((gy,)),
+            dma((6, 2)),
+            dma((6, 2)),
+            dma,
+            dma,
+            dma,
+            dma,
         ],
         compiler_params=pltpu.CompilerParams(
             collective_id=0, has_side_effects=True, vmem_limit_bytes=63 * 2**20 + 2**19

time: 58 us -> 53.9 us (0.929)
  Pallas kernels: 55.8 us -> 51.7 us
    pallas_call x1, Pallas kernels: 55.8 us -> 51.7 us  [shards(): pl.pallas_call(functools.partial(kernel, gx, gy), out_shape=jax.ShapeDtyp...]
where the time goes in v4:
time: 53.9 us; the launch traced here: 53.7 us
  Pallas kernels  51.7 us (96%)
  local copies, waits for them, and re-layouts  2.06 us (4%)
    pallas_call x1, Pallas kernels, shards(): pl.pallas_call(functools.partial(kernel, gx, gy), out_shape=jax.ShapeDtyp...  51.7 us
    unnamed x1, local copies, waits for them, and re-layouts  2.06 us

profile of v4, /device:TPU:0, one launch (start us, length us, event | category | flops | bytes accessed | tf_op | source)
XLA Modules:
  0.0 53.7 jit_solution(7958381566224570221)
XLA Ops:
  0.0 51.7 %precondition.1 = f32[3,32,8,256]{3,2,1,0:T(8,128)} custom-call(f32[3,32,8,256]{3,2,1,0:T(8,128)} %rhs.1, f32[6,3,3,32,8,256]{5,4,3,2,1,0:T(8,128)} %couplings.1, f32[3,3,32,8,256]{4,3,2,1,0:T(8,128)} %pivots_in.1, s32[32,8,256]{2,1,0:T(8,128)} %colours_in.1, s32[1,1024]{1,0:T(1,128)} %bitcast.9, s32[1,1024]{1,0:T(1,128)} %bitcast.10, s32[1,1024]{1,0:T(1,128)} %bitcast.11, ...), custom_call_target="tpu_custom_call" | custom-call | tf_op jit(solution)/shard_map/precondition/pallas_call | solution.py:522
  51.7 2.1 %copy.14 = f32[3,32,8,256]{3,2,1,0:T(8,128)} copy(f32[3,32,8,256]{3,2,1,0:T(8,128)} %precondition.1) | data formatting | bytes 1572864

commit v5 on v4

--- a/solution.py
+++ b/solution.py
@@ -90,6 +90,7 @@
     values,
     load_sem,
     small_sem,
+    store_sem,
     x_send,
     x_recv,
     y_send,
@@ -250,22 +251,24 @@
                 y_add[side, i] = sum(cy_edge[side, i, j] * yhalo[slot, side, j] for j in range(3))
 
     def interior(z, carry):
+        here = [fld[j, z + 1] for j in range(3)]
+        shifted = []
+        for j in range(3):
+            shifted += [
+                (2, j, jnp.where(row == 0, 0.0, pltpu.roll(here[j], 1, 0))),
+                (3, j, jnp.where(row == cy - 1, 0.0, pltpu.roll(here[j], cy - 1, 0))),
+                (0, j, jnp.where(wide_lane == 0, 0.0, pltpu.roll(here[j], 1, 1))),
+                (1, j, jnp.where(wide_lane == cx - 1, 0.0, pltpu.roll(here[j], cx - 1, 1))),
+            ]
         total = [upper[i, z] for i in range(3)]
         for j in range(3):
-            here = fld[j, z + 1]
-            beside = (
-                jnp.where(wide_lane == 0, 0.0, pltpu.roll(here, 1, 1)),
-                jnp.where(wide_lane == cx - 1, 0.0, pltpu.roll(here, cx - 1, 1)),
-                jnp.where(row == 0, 0.0, pltpu.roll(here, 1, 0)),
-                jnp.where(row == cy - 1, 0.0, pltpu.roll(here, cy - 1, 0)),
-                fld[j, z],
-                fld[j, z + 2],
-            )
+            below, above = fld[j, z], fld[j, z + 2]
             for i in range(3):
-                for k in range(6):
-                    total[i] = total[i] - coup[k, i, j, z] * beside[k]
+                total[i] = total[i] - coup[4, i, j, z] * below
+                total[i] = total[i] - coup[5, i, j, z] * above
         for i in range(3):
-            acc[i, z] = total[i]
+            across = sum(coup[k, i, j, z] * beside for k, j, beside in shifted)
+            acc[i, z] = total[i] - across
         return carry
 
     def finish(turn, colour, z, packs):
@@ -345,7 +348,7 @@
 
     def one_turn(turn, carry):
         colour = 3 - jnp.abs(turn - 3)
-        lax.fori_loop(0, nz, interior, 0, unroll=4)
+        lax.fori_loop(0, nz, interior, 0, unroll=8)
         take_halo(turn - 1)
         packs = sweep_layers(turn, functools.partial(finish, turn, colour))
 
@@ -374,7 +377,7 @@
         terms[:, at] = jnp.sum(jnp.where(row_index == there, term, 0.0), axis=0, keepdims=True)
         return carry
 
-    lax.fori_loop(0, perfs // chunk, read_terms, 0)
+    lax.fori_loop(0, perfs // chunk, read_terms, 0, unroll=2)
     sums = sum(dot_nt(hot_hi[...], hot_lo[...] * part) for part in parts_of(terms[...]))
     totals[...] = sums.reshape(totals.shape)
 
@@ -469,10 +472,12 @@
         read = sum(dot_nn(part, column) for part in table_parts)
         terms[:, at] = jnp.sum(read * hot_hi[:, at].astype(F32), axis=0, keepdims=True)
     at_perfs = terms[...]
+    stores = [pltpu.make_async_copy(acc.at[u], out.at[u], store_sem.at[u]) for u in range(3)]
     for u in range(3):
         weights = parts_of(ret[u : u + 1, :] * at_perfs, 2)
         change = sum(dot_nt(hot_r[...], hot_x[...] * part) for part in weights)
-        out[u] = fld[u, 1 : nz + 1] - change.reshape(nz, cy, cx)
+        acc[u] = fld[u, 1 : nz + 1] - change.reshape(nz, cy, cx)
+        stores[u].start()
 
     for done in range(6):
         for pair in (x_copies(done), y_copies(done, slice(None))):
@@ -480,6 +485,8 @@
                 pl.when(inside)(copy.wait_send)
     sent_totals(1, count - 1).wait_send()
     all_values.wait_send()
+    for store in stores:
+        store.wait()
 
 
 def shards(
@@ -523,7 +530,7 @@
         functools.partial(kernel, gx, gy),
         out_shape=jax.ShapeDtypeStruct(rhs_field.shape, F32),
         in_specs=[hbm] * len(operands),
-        out_specs=pl.BlockSpec(memory_space=pltpu.VMEM),
+        out_specs=hbm,
         scratch_shapes=[pltpu.VMEM(x.shape, x.dtype) for x in operands]
         + [
             pltpu.VMEM((3, nz + 2, cy, cx), F32),
@@ -547,6 +554,7 @@
             pltpu.VMEM((gx * gy, per_owner, LANES), F32),
             dma((6,)),
             dma((11,)),
+            dma((3,)),
             dma((6, 2)),
             dma((6, 2)),
             dma((6, 2)),

time: 53.9 us -> 53 us (0.983)
  Pallas kernels: 51.7 us -> 50.8 us
    pallas_call x1, Pallas kernels: 51.7 us -> 50.8 us  [shards(): pl.pallas_call(functools.partial(kernel, gx, gy), out_shape=jax.ShapeDtyp...]
where the time goes in v5:
time: 53 us; the launch traced here: 52.9 us
  Pallas kernels  50.8 us (96%)
  local copies, waits for them, and re-layouts  2.06 us (4%)
    pallas_call x1, Pallas kernels, shards(): pl.pallas_call(functools.partial(kernel, gx, gy), out_shape=jax.ShapeDtyp...  50.8 us
    unnamed x1, local copies, waits for them, and re-layouts  2.06 us

profile of v5, /device:TPU:0, one launch (start us, length us, event | category | flops | bytes accessed | tf_op | source)
XLA Modules:
  0.0 52.9 jit_solution(2636540234149103932)
XLA Ops:
  0.0 50.8 %precondition.1 = f32[3,32,8,256]{3,2,1,0:T(8,128)} custom-call(f32[3,32,8,256]{3,2,1,0:T(8,128)} %rhs.1, f32[6,3,3,32,8,256]{5,4,3,2,1,0:T(8,128)} %couplings.1, f32[3,3,32,8,256]{4,3,2,1,0:T(8,128)} %pivots_in.1, s32[32,8,256]{2,1,0:T(8,128)} %colours_in.1, s32[1,1024]{1,0:T(1,128)} %bitcast.9, s32[1,1024]{1,0:T(1,128)} %bitcast.10, s32[1,1024]{1,0:T(1,128)} %bitcast.11, ...), custom_call_target="tpu_custom_call" | custom-call | tf_op jit(solution)/shard_map/precondition/pallas_call | solution.py:529
  50.8 2.1 %copy.14 = f32[3,32,8,256]{3,2,1,0:T(8,128)} copy(f32[3,32,8,256]{3,2,1,0:T(8,128)} %precondition.1) | data formatting | bytes 1572864
